TPU v7x, 128 devices: a whole 4x4x4 slice. The times are simulated.
128 devices in a mesh: lon: 16 (over z, x_lo, core), lat: 8 (over x_hi, y).
Axes of the slice: x: 4 (x_hi: 2, x_lo: 2; x = x_hi * 2 + x_lo), y: 4, z: 4, core: 2. Of those that a mesh axis runs over, the one named last changes fastest.
Arguments:
- block_input: bfloat16 [2, 384, 384, 512], P(None, 'lat', 'lon'), may hold values from -6 to 6
- gain: float32 [512], replicated, may hold values from 0.25 to 1.75
- w_qkv: bfloat16 [512, 1536], replicated
- w_out: bfloat16 [512, 512], replicated, may hold values from -0.25 to 0.25
- w_dec: bfloat16 [512, 80], replicated, may hold values from -0.25 to 0.25
- g_points: bfloat16 [131072, 80], P(('lat', 'lon')), may hold values from -6 to 6
- slot_point: int32 [1024, 512], P(('lat', 'lon')), may hold values from 0 to 1023
- slot_cell: int32 [1024, 512], P(('lat', 'lon')), may hold values from 0 to 2303
- slot_weight: float32 [1024, 512], P(('lat', 'lon')), may hold values from 0.25 to 1
- pair_count: int32 [1024], P(('lat', 'lon')), may hold values from 128 to 512, as said below
Outputs:
- grad_x: bfloat16 [2, 384, 384, 512], P(None, 'lat', 'lon')
- grad_qkv: float32 [512, 1536], replicated
- grad_out: float32 [512, 512], replicated
- grad_dec: float32 [512, 80], replicated
- grad_gain: float32 [512], replicated
Inputs may be any that keep to these rules, and one draw needn't show every extreme that they name: slot_point indexes the owner's 1024 points. slot_cell indexes the source's 2304 local cells. `pair_count`: every device sends exactly 512 live entries to at least one band.
All inputs are finite; a program needn't handle non-finite values.
Results may differ from a plain program's by a relative error of at most 0.02.
The roundings to bfloat16 on the way count: a program that leaves them out, or rounds other values in their place, can miss the bound.
Values may be sent and summed in bfloat16 or wider, within the bound.
A program may use at most 192 MiB of HBM per device.

v0:
```python
import jax
import jax.numpy as jnp
from jax import lax
from jax.sharding import PartitionSpec as P

HEADS = 8
HD = 64
LEV = 2
WA = 6
WO = 12


def shifted_2(value, axis, steps):
    count = lax.axis_size(axis)
    pairs = [(source, (source + steps) % count) for source in range(count)]
    return lax.ppermute(value, axis, pairs)


def prod(form, left, right):
    return jnp.einsum(form, left, right, preferred_element_type=jnp.float32)


def to_windows(tile):
    levels, lat_rows, lon_cols, width = tile.shape
    blocks = tile.reshape(levels, lat_rows // WA, WA, lon_cols // WO, WO, width).transpose(
        1, 3, 0, 2, 4, 5
    )
    return blocks.reshape(lat_rows // WA, lon_cols // WO, levels * WA * WO, width)


def from_windows(blocks):
    lat_blocks, lon_blocks, window, width = blocks.shape
    tile = blocks.reshape(lat_blocks, lon_blocks, LEV, WA, WO, width).transpose(2, 0, 3, 1, 4, 5)
    return tile.reshape(LEV, lat_blocks * WA, lon_blocks * WO, width)


def attend_forward(windows, gain, w_qkv, w_out):
    count, window, width = windows.shape
    inputs = windows.astype(jnp.float32)
    rscale = lax.rsqrt(jnp.mean(inputs * inputs, -1, keepdims=True) + 1e-06)
    normed = (inputs * rscale * gain).astype(jnp.bfloat16)
    qkv = jnp.dot(normed.reshape(count * window, width), w_qkv, preferred_element_type=jnp.float32)
    qkv = qkv.astype(jnp.bfloat16).reshape(count, window, 3, HEADS, HD)
    query, keys, values = (qkv[:, :, 0], qkv[:, :, 1], qkv[:, :, 2])
    scores = prod("wqhe,wkhe->whqk", query, keys) * HD ** (-0.5)
    probs = jax.nn.softmax(scores, -1)
    probs_b = probs.astype(jnp.bfloat16)
    attended = (
        prod("whqk,wkhe->wqhe", probs_b, values).astype(jnp.bfloat16).reshape(count * window, width)
    )
    hidden = (
        inputs.reshape(count * window, width)
        + jnp.dot(attended, w_out, preferred_element_type=jnp.float32)
    ).astype(jnp.bfloat16)
    return (rscale, normed, query, keys, values, probs, probs_b, attended, hidden)


def attend_backward(windows, saved, dhid, gain, w_qkv, w_out):
    rscale, normed, query, keys, values, probs, probs_b, attended, hidden = saved
    count, window, width = windows.shape
    dhid_b = dhid.astype(jnp.bfloat16)
    grad_out = jnp.dot(attended.T, dhid_b, preferred_element_type=jnp.float32)
    datt = (
        jnp.dot(dhid_b, w_out.T, preferred_element_type=jnp.float32)
        .astype(jnp.bfloat16)
        .reshape(count, window, HEADS, HD)
    )
    dprob = prod("wqhe,wkhe->whqk", datt, values)
    dvalue = prod("whqk,wqhe->wkhe", probs_b, datt)
    dscore = probs * (dprob - jnp.sum(probs * dprob, -1, keepdims=True)) * HD ** (-0.5)
    dscore_b = dscore.astype(jnp.bfloat16)
    dquery = prod("whqk,wkhe->wqhe", dscore_b, keys)
    dkey = prod("whqk,wqhe->wkhe", dscore_b, query)
    dqkv = (
        jnp.stack([dquery, dkey, dvalue], 2).astype(jnp.bfloat16).reshape(count * window, 3 * width)
    )
    grad_qkv = jnp.dot(
        normed.reshape(count * window, width).T, dqkv, preferred_element_type=jnp.float32
    )
    dnormed = jnp.dot(dqkv, w_qkv.T, preferred_element_type=jnp.float32)
    inputs = windows.reshape(count * window, width).astype(jnp.float32)
    rflat = rscale.reshape(count * window, 1)
    grad_gain = jnp.sum(dnormed * inputs * rflat, 0)
    dscaled = dnormed * gain
    dshift = dhid + rflat * (
        dscaled - inputs * rflat * rflat * jnp.mean(dscaled * inputs, -1, keepdims=True)
    )
    return (dshift, grad_qkv, grad_out, grad_gain)


def window_part(blocks, dhid_blocks, gain, w_qkv, w_out, grad_rows):
    lat_blocks, lon_blocks, window, width = blocks.shape
    flat = blocks.reshape(lat_blocks * lon_blocks, window, width)
    saved = attend_forward(flat, gain, w_qkv, w_out)
    dshift, g_qkv, g_out, g_gain = attend_backward(
        flat, saved, dhid_blocks.reshape(-1, width), gain, w_qkv, w_out
    )
    g_dec = jnp.dot(
        saved[8].T, grad_rows.reshape(-1, grad_rows.shape[-1]), preferred_element_type=jnp.float32
    )
    back = dshift.astype(jnp.bfloat16).reshape(lat_blocks, lon_blocks, window, width)
    return (back, g_qkv, g_out, g_gain, g_dec)


def body(
    block_input, gain, w_qkv, w_out, w_dec, g_points, slot_point, slot_cell, slot_weight, pair_count
):
    levels, lat_rows, lon_cols, width = block_input.shape
    shift_cols = WO // 2
    incoming = shifted_2(block_input[:, :, :shift_cols], "lon", -1)
    shifted = jnp.concatenate([block_input[:, :, shift_cols:], incoming], axis=2)
    blocks = to_windows(shifted)
    lat_blocks, lon_blocks, window, _ = blocks.shape
    slots = slot_point.shape[1]
    bands = lax.axis_size("lat")
    outputs = g_points.shape[1]
    every_point = lax.all_gather(g_points, "lat", axis=0, tiled=True)
    all_lists, all_counts = (
        lax.all_gather(slot_point, "lat", axis=0, tiled=True),
        lax.all_gather(pair_count, "lat", axis=0, tiled=True),
    )
    all_weights = lax.all_gather(slot_weight, "lat", axis=0, tiled=True)
    band = lax.axis_index("lat")
    own_lists = lax.dynamic_index_in_dim(
        all_lists.reshape(bands, bands, slots), band, 1, keepdims=False
    )
    own_weights = lax.dynamic_index_in_dim(
        all_weights.reshape(bands, bands, slots), band, 1, keepdims=False
    )
    own_counts = lax.dynamic_index_in_dim(all_counts.reshape(bands, bands), band, 1, keepdims=False)
    offsets = (jnp.arange(bands, dtype=jnp.int32) * g_points.shape[0])[:, None]
    live = jnp.arange(slots)[None, :] < own_counts[:, None]
    picked = jnp.take(every_point, own_lists + offsets, axis=0)
    arrived = jnp.where(
        live[..., None], own_weights[..., None] * picked.astype(jnp.float32), 0.0
    ).astype(jnp.bfloat16)
    tokens = lat_blocks * lon_blocks * window
    grad_tok = (
        jnp.zeros((tokens, outputs), jnp.float32)
        .at[slot_cell.reshape(-1)]
        .add(arrived.reshape(-1, outputs).astype(jnp.float32))
    )
    grad_tok = grad_tok.astype(jnp.bfloat16)
    dhid = jnp.dot(grad_tok, w_dec.T, preferred_element_type=jnp.float32).reshape(
        lat_blocks, lon_blocks, window, width
    )
    grad_blocks = grad_tok.reshape(lat_blocks, lon_blocks, window, outputs)
    all_back, g_qkv, g_out, g_gain, g_dec = window_part(
        blocks, dhid, gain, w_qkv, w_out, grad_blocks
    )
    tile = from_windows(all_back)
    outgoing = tile[:, :, lon_cols - shift_cols :]
    arriving = shifted_2(outgoing, "lon", 1)
    grad_x = jnp.concatenate([arriving, tile[:, :, : lon_cols - shift_cols]], axis=2)
    g_qkv, g_out, g_dec, g_gain = lax.psum((g_qkv, g_out, g_dec, g_gain), ("lat", "lon"))
    return (grad_x, g_qkv, g_out, g_dec, g_gain)


def solution(mesh):
    placed = (
        P(None, "lat", "lon", None),
        P(),
        P(),
        P(),
        P(),
        P(("lat", "lon"), None),
        P(("lat", "lon"), None),
        P(("lat", "lon"), None),
        P(("lat", "lon"), None),
        P(("lat", "lon")),
    )
    return jax.shard_map(
        body,
        mesh=mesh,
        in_specs=placed,
        out_specs=(P(None, "lat", "lon", None), P(), P(), P(), P()),
        check_vma=False,
    )
```

profile of v0, /device:TPU:1, one launch (start us, length us, event | category | flops | bytes accessed | tf_op | source)
XLA Modules:
  0.0 639.2 jit_solution(14699128638186073683)
XLA Ops:
  7.3 1.9 copy.69
  12.1 4.4 slice.21
  16.5 28.9 %all_gather.13 = f32[64,512]{1,0:T(8,128)S(1)} all-gather(f32[8,512]{1,0:T(8,128)S(1)} %copy-done.12), channel_id=1, replica_groups=mesh['lon'=16,'lat'=8] {'lat'}, dimensions={0}, use_global_device_ids=true | all-gather | bytes 147456 | tf_op jit(solution)/shard_map/all_gather | solution.py:122
  45.3 28.1 %all_gather.14 = s32[64,512]{1,0:T(8,128)S(1)} all-gather(s32[8,512]{1,0:T(8,128)S(1)} %copy-done.13), channel_id=1, replica_groups=mesh['lon'=16,'lat'=8] {'lat'}, dimensions={0}, use_global_device_ids=true | all-gather | bytes 147456 | tf_op jit(solution)/shard_map/all_gather | solution.py:119
  75.3 10.0 %all-reduce.1 = s32[8,8]{1,0:T(8,128)S(1)} all-reduce(s32[8,8]{1,0:T(8,128)S(1)} %reshape.222), channel_id=1, replica_groups=mesh['lon'=16,'lat'=8] {'lat'}, use_global_device_ids=true, to_apply=%add | all-reduce | flops 64 | bytes 512
  86.0 2.5 maximum_convert_fusion.1
  88.5 4.1 copy.72
  92.6 4.1 copy.116
  96.6 2.6 fusion.17
  99.7 7.3 %reshape.229 = f32[2304,512]{1,0:T(8,128)} reshape(f32[8,2,2,6,12,512]{5,4,3,2,1,0:T(8,128)} %bitcast.94) | data formatting | bytes 9437184 | tf_op jit(solution)/shard_map/convert_element_type | solution.py:39
  107.1 8.4 %convolution_convert_fusion = bf16[2304,1536]{1,0:T(8,128)(2,1)} fusion(bf16[512,1536]{1,0:T(8,128)(2,1)S(1)} %copy-done, f32[2304,512]{1,0:T(8,128)} %reshape.229, f32[512]{0:T(512)S(1)} %copy-done.15, f32[2304]{0:T(1024)S(1)} %rsqrt.17), kind=kOutput, calls=%fused_computation.13 | convolution fusion | flops 3630956544 | bytes 13380608 | tf_op jit(solution)/shard_map/dot_general | solution.py:42
  115.5 18.0 %reshape.255 = bf16[16,144,3,8,64]{4,3,2,1,0:T(8,128)(2,1)} reshape(bf16[2304,1536]{1,0:T(8,128)(2,1)} %convolution_convert_fusion) | data formatting | bytes 14155776 | tf_op jit(solution)/shard_map/reshape | solution.py:43
  133.6 13.1 %fusion.75 = (bf16[16,144,1,8,64]{4,3,2,1,0:T(8,128)(2,1)}, bf16[16,144,1,8,64]{4,3,2,1,0:T(8,128)(2,1)}, bf16[16,144,1,8,64]{4,3,2,1,0:T(8,128)(2,1)}) fusion(bf16[16,144,3,8,64]{4,3,2,1,0:T(8,128)(2,1)} %reshape.255), kind=kLoop, calls=%fused_computation.89 | loop fusion | bytes 14155776 | tf_op jit(solution)/shard_map/slice | solution.py:44
  146.6 7.8 %copy.107 = bf16[16,144,1,8,64]{1,4,3,0,2:T(8,128)(2,1)} copy(bf16[16,144,1,8,64]{4,3,2,1,0:T(8,128)(2,1)} %get-tuple-element.28) | data formatting | bytes 4718592
  154.4 7.8 %copy.106 = bf16[16,144,1,8,64]{1,4,3,0,2:T(8,128)(2,1)} copy(bf16[16,144,1,8,64]{4,3,2,1,0:T(8,128)(2,1)} %get-tuple-element.29) | data formatting | bytes 4718592
  162.1 12.6 %fusion.29 = f32[16,8,144,144]{2,3,1,0:T(8,128)} fusion(bf16[16,144,1,8,64]{1,4,3,0,2:T(8,128)(2,1)} %copy.107, bf16[16,144,1,8,64]{1,4,3,0,2:T(8,128)(2,1)} %copy.106), kind=kOutput, calls=%fused_computation.39 | convolution fusion | flops 339738624 | bytes 15335424 | tf_op jit(solution)/shard_map/wqhe,wkhe->whqk/dot_general | solution.py:20
  174.8 21.4 %fusion.76 = (f32[16,8,144]{2,1,0:T(8,128)S(1)}, f32[16,8,144,144]{2,3,1,0:T(8,128)}) fusion(f32[16,8,144,144]{2,3,1,0:T(8,128)} %fusion.29), kind=kOutput, calls=%fused_computation.90 | output fusion | flops 10616975 | bytes 21307392 | tf_op jit(solution)/shard_map/sub | solution.py:46
  196.1 8.0 %copy.108 = bf16[16,144,1,8,64]{1,4,3,0,2:T(8,128)(2,1)} copy(bf16[16,144,1,8,64]{4,3,2,1,0:T(8,128)(2,1)} %get-tuple-element.27) | data formatting | bytes 4718592
  204.1 5.0 fusion.19
  209.1 2.6 copy.91
  211.7 5.0 convert_element_type.104
  216.7 11.2 %convert_bitcast_fusion = bf16[16,144,8,64]{1,3,2,0:T(8,128)(2,1)} fusion(bf16[16,144,1,8,64]{1,4,3,0,2:T(8,128)(2,1)} %copy.108, f32[16,8,144,144]{2,3,1,0:T(8,128)} %get-tuple-element.31, f32[16,8,144]{2,1,0:T(8,128)S(1)} %get-tuple-element.30), kind=kOutput, calls=%fused_computation.43 | convolution fusion | flops 346226688 | bytes 15409152 | tf_op jit(solution)/shard_map/whqk,wkhe->wqhe/dot_general | solution.py:20
  227.9 6.7 %copy.93 = bf16[16,144,8,64]{1,0,3,2:T(8,128)(2,1)} copy(bf16[16,144,8,64]{1,3,2,0:T(8,128)(2,1)} %convert_bitcast_fusion) | data formatting | bytes 4718592 | tf_op jit(solution)/shard_map/convert_element_type | solution.py:49
  234.6 7.9 %reshape.228 = bf16[2304,512]{0,1:T(8,128)(2,1)} reshape(bf16[16,144,8,64]{1,0,3,2:T(8,128)(2,1)} %copy.93) | data formatting | bytes 4718592 | tf_op jit(solution)/shard_map/reshape | solution.py:49
  242.6 48.8 %scatter_custom_fusion = f32[2304,80]{1,0:T(8,128)S(1)} fusion(s32[4096]{0:T(1024)S(1)} %bitcast.107, f32[]{:T(128)} %constant.17.clone.1, f32[4096]{0:T(1024)S(1)} %bitcast.104, pred[4096]{0:T(1024)(128)(4,1)S(1)} %compare_and_fusion, pred[4096]{0:T(1024)(128)(4,1)S(1)} %bitcast.105, bf16[]{:T(256)} %constant.29.clone.1, ...), kind=kCustom, calls=%fused_computation.51 | custom fusion | flops 1966080 | bytes 2876928 | tf_op jit(solution)/shard_map/scatter-add | solution.py:141
  292.2 2.2 copy-done.2
  294.4 2.9 convolution_convert_fusion.1
  297.3 7.4 %reshape.256 = bf16[16,144,8,64]{3,2,1,0:T(8,128)(2,1)} reshape(bf16[2304,512]{1,0:T(8,128)(2,1)} %convolution_convert_fusion.1) | data formatting | bytes 4718592 | tf_op jit(solution)/shard_map/reshape | solution.py:66
  304.7 7.8 %copy.83 = bf16[16,144,8,64]{1,3,2,0:T(8,128)(2,1)} copy(bf16[16,144,8,64]{3,2,1,0:T(8,128)(2,1)} %reshape.256) | data formatting | bytes 4718592 | tf_op jit(solution)/shard_map/reshape | solution.py:66
  312.5 11.5 %fusion.43 = bf16[16,144,1,8,64]{1,4,3,0,2:T(8,128)(2,1)} fusion(bf16[16,144,8,64]{1,3,2,0:T(8,128)(2,1)} %copy.83, f32[16,8,144,144]{2,3,1,0:T(8,128)} %get-tuple-element.31, f32[16,8,144]{2,1,0:T(8,128)S(1)} %get-tuple-element.30), kind=kOutput, calls=%fused_computation.46 | convolution fusion | flops 345047040 | bytes 15409152 | tf_op jit(solution)/shard_map/whqk,wqhe->wkhe/dot_general | solution.py:20
  324.1 11.4 %fusion.26 = f32[16,8,144,144]{2,3,1,0:T(8,128)} fusion(bf16[16,144,8,64]{1,3,2,0:T(8,128)(2,1)} %copy.83, bf16[16,144,1,8,64]{1,4,3,0,2:T(8,128)(2,1)S(1)} %copy-done.3), kind=kOutput, calls=%fused_computation.36 | convolution fusion | flops 339738624 | bytes 15335424 | tf_op jit(solution)/shard_map/wqhe,wkhe->whqk/dot_general | solution.py:20
  335.4 28.1 %fusion.38 = bf16[16,144,1,8,64]{1,4,3,0,2:T(8,128)(2,1)} fusion(f32[16,8,144,144]{2,3,1,0:T(8,128)} %fusion.26, bf16[16,144,1,8,64]{1,4,3,0,2:T(8,128)(2,1)} %copy.107, f32[16,8,144,144]{2,3,1,0:T(8,128)} %get-tuple-element.31, f32[16,8,144]{2,1,0:T(8,128)S(1)} %get-tuple-element.30), kind=kOutput, calls=%fused_computation.45 | convolution fusion | flops 358336640 | bytes 26025984 | tf_op jit(solution)/shard_map/whqk,wqhe->wkhe/dot_general | solution.py:20
  363.6 27.8 %fusion.33 = bf16[16,144,1,8,64]{1,4,3,0,2:T(8,128)(2,1)} fusion(f32[16,8,144,144]{2,3,1,0:T(8,128)} %fusion.26, bf16[16,144,1,8,64]{1,4,3,0,2:T(8,128)(2,1)} %copy.106, f32[16,8,144,144]{2,3,1,0:T(8,128)} %get-tuple-element.31, f32[16,8,144]{2,1,0:T(8,128)S(1)} %get-tuple-element.30), kind=kOutput, calls=%fused_computation.44 | convolution fusion | flops 358336640 | bytes 26025984 | tf_op jit(solution)/shard_map/whqk,wkhe->wqhe/dot_general | solution.py:20
  391.4 5.4 fusion.55
  396.8 5.5 fusion.54
  402.3 5.9 maximum_convert_fusion
  408.3 9.0 %copy.88 = bf16[16,144,3,8,64]{1,0,4,3,2:T(8,128)(2,1)} copy(bf16[16,144,3,8,64]{1,4,3,0,2:T(8,128)(2,1)S(1)} %maximum_convert_fusion) | data formatting | bytes 14155776 | tf_op jit(solution)/shard_map/convert_element_type | solution.py:75
  417.3 21.0 %convert_element_type.101 = bf16[2304,1536]{0,1:T(8,128)(2,1)} reshape(bf16[16,144,3,8,64]{1,0,4,3,2:T(8,128)(2,1)} %copy.88) | data formatting | bytes 14155776 | tf_op jit(solution)/shard_map/convert_element_type | solution.py:75
  438.3 11.0 %multiply_reduce_fusion.2 = (f32[512]{0:T(512)S(1)}, f32[2304]{0:T(1024)S(1)}, f32[2304,512]{1,0:T(8,128)}) fusion(f32[2304,512]{1,0:T(8,128)} %reshape.229, f32[2304]{0:T(1024)S(1)} %copy-done.11, f32[512]{0:T(512)S(1)} %copy-done.15, bf16[2304,1536]{0,1:T(8,128)(2,1)} %convert_element_type.101, bf16[512,1536]{1,0:T(8,128)(2,1)S(1)} %copy-done), kind=kOutput, calls=%fused_computation.25 | convolution fusion | flops 3630953728 | bytes 18110464 | tf_op jit(solution)/shard_map/dot_general | solution.py:80
  449.2 5.6 fusion.77
  454.9 7.3 %add_convert_fusion = bf16[2304,512]{1,0:T(8,128)(2,1)} fusion(f32[2304,512]{1,0:T(8,128)} %copy-done.2, f32[2304,512]{1,0:T(8,128)} %get-tuple-element.32, f32[2304,512]{1,0:T(8,128)} %reshape.229, f32[2304]{0:T(1024)S(1)} %broadcast_multiply_fusion, f32[512]{0:T(512)S(1)} %copy-done.15, f32[2304]{0:T(1024)S(1)} %copy-done.11), kind=kLoop, calls=%fused_computation.26 | loop fusion | flops 9437184 | bytes 16535552 | tf_op jit(solution)/shard_map/convert_element_type | solution.py:101
  462.2 5.1 reshape_reshape.4
  467.3 5.8 copy.89
  474.3 15.6 %collective-permute-start.1 = (bf16[2,48,6,512]{3,0,2,1:T(2,128)(2,1)}, bf16[2,48,6,512]{3,0,2,1:T(2,128)(2,1)}, u32[]{:S(2)}, u32[]{:S(2)}) collective-permute-start(bf16[2,48,6,512]{3,0,2,1:T(2,128)(2,1)} %slice.33), channel_id=1, source_target_pairs={{0,8},{8,16},{16,24},{24,32},{32,40},{40,48},{48,56},{56,64},{64,7... | collective-permute-start | bytes 1769480 | tf_op jit(solution)/shard_map/ppermute | solution.py:16
  491.1 68.2 %psum.31 = f32[512]{0:T(512)} all-reduce(f32[512]{0:T(512)S(1)} %get-tuple-element.20), channel_id=1, replica_groups=mesh['lon'=16,'lat'=8] {'lat','lon'}, use_global_device_ids=true, to_apply=%region_10.11 | all-reduce | flops 512 | bytes 4096 | tf_op jit(solution)/shard_map/psum | solution.py:155
  559.4 4.1 pad_maximum_fusion
  565.2 61.4 %all-reduce.5.cloned.1.call-done = (f32[512,1536]{1,0:T(8,128)}, f32[512,512]{1,0:T(8,128)}, f32[512,80]{0,1:T(8,128)}) async-done(((f32[512,1536]{1,0:T(8,128)}, f32[512,512]{1,0:T(8,128)}, f32[512,80]{0,1:T(8,128)}), (f32[512,1536]{1,0:T(8,128)}, f32[512,512]{1,0:T(8,128)}, f32[512,80]{0,1:T(8,128)})) %all-reduce.5.cloned.1.call-update) | async-done | bytes 4358160 | tf_op jit(solution)/shard_map/psum | solution.py:155
  626.7 3.9 copy.121
  (74 shorter events, 12.0 us)
Async XLA Ops:
  7.2 99.9 %copy-start = (bf16[512,1536]{1,0:T(8,128)(2,1)S(1)}, bf16[512,1536]{1,0:T(8,128)(2,1)}, u32[]{:S(2)}) copy-start(bf16[512,1536]{1,0:T(8,128)(2,1)} %param.12) | copy-start | bytes 4718596
  7.2 66.5 %copy-start.17 = (u32[128]{0:T(128)S(1)}, u32[128]{0:T(128)}, u32[]{:S(2)}) copy-start(u32[128]{0:T(128)} %constant.60) | copy-start | bytes 1540
  7.2 9.2 %copy-start.14 = (s32[8,512]{1,0:T(8,128)S(1)}, s32[8,512]{1,0:T(8,128)}, u32[]{:S(2)}) copy-start(s32[8,512]{1,0:T(8,128)} %param.17) | copy-start | bytes 49156
  7.2 9.3 %copy-start.12 = (f32[8,512]{1,0:T(8,128)S(1)}, f32[8,512]{1,0:T(8,128)}, u32[]{:S(2)}) copy-start(f32[8,512]{1,0:T(8,128)} %param.18) | copy-start | bytes 49156
  7.2 38.1 %copy-start.13 = (s32[8,512]{1,0:T(8,128)S(1)}, s32[8,512]{1,0:T(8,128)}, u32[]{:S(2)}) copy-start(s32[8,512]{1,0:T(8,128)} %param.16) | copy-start | bytes 49156
  7.2 67.7 %copy-start.16 = (s32[8]{0:T(128)S(1)}, s32[8]{0:T(128)}, u32[]{:S(2)}) copy-start(s32[8]{0:T(128)} %param.19) | copy-start | bytes 100
  7.2 235.4 %all-gather.2.cloned.1.call-start = ((), (), s32[]{:S(2)}) async-start(), calls=%async_computation | async-start | bytes 2359296 | tf_op jit(solution)/shard_map/all_gather | solution.py:117
  9.2 617.5 %all-reduce.5.cloned.1.call-start = ((), (), s32[]{:S(2)}) async-start(), calls=%async_computation.1 | async-start | bytes 8716288 | tf_op jit(solution)/shard_map/psum | solution.py:155
  10.6 75.0 %collective-permute-start = (bf16[2,48,6,512]{3,1,2,0:T(8,128)(2,1)S(1)}, bf16[2,48,6,512]{3,1,2,0:T(8,128)(2,1)S(1)}, u32[]{:S(2)}, u32[]{:S(2)}) collective-permute-start(bf16[2,48,6,512]{3,1,2,0:T(8,128)(2,1)S(1)} %copy.105), channel_id=1, source_target_pairs={{0,120},{8,0},{16,8},{24,16},{32,24},{40,32},{48,40},{56,48},{64,5... | collective-permute-start | bytes 1769480 | tf_op jit(solution)/shard_map/ppermute | solution.py:16
  92.6 4.1 copy-start.1
  99.7 7.4 %copy-start.15 = (f32[512]{0:T(512)S(1)}, f32[512]{0:T(512)}, u32[]{:S(2)}) copy-start(f32[512]{0:T(512)} %param.11) | copy-start | bytes 6148
  107.1 8.5 %copy-start.10 = (f32[2304]{0:T(1024)}, f32[2304]{0:T(1024)S(1)}, u32[]{:S(2)}) copy-start(f32[2304]{0:T(1024)S(1)} %rsqrt.17) | copy-start | bytes 27652
  234.6 56.8 %copy-start.9 = (bf16[512,80]{0,1:T(8,128)(2,1)S(1)}, bf16[512,80]{0,1:T(8,128)(2,1)}, u32[]{:S(2)}) copy-start(bf16[512,80]{0,1:T(8,128)(2,1)} %param.14) | copy-start | bytes 245764
  242.6 51.8 %copy-start.7 = (bf16[512,512]{1,0:T(8,128)(2,1)S(1)}, bf16[512,512]{1,0:T(8,128)(2,1)}, u32[]{:S(2)}) copy-start(bf16[512,512]{1,0:T(8,128)(2,1)} %param.13) | copy-start | bytes 1572868
  292.2 2.2 copy-start.2
  312.5 11.5 %copy-start.3 = (bf16[16,144,1,8,64]{1,4,3,0,2:T(8,128)(2,1)S(1)}, bf16[16,144,1,8,64]{1,4,3,0,2:T(8,128)(2,1)}, u32[]{:S(2)}) copy-start(bf16[16,144,1,8,64]{1,4,3,0,2:T(8,128)(2,1)} %copy.108) | copy-start | bytes 7077892
  417.3 21.0 %copy-start.11 = (f32[2304]{0:T(1024)S(1)}, f32[2304]{0:T(1024)}, u32[]{:S(2)}) copy-start(f32[2304]{0:T(1024)} %copy-done.10) | copy-start | bytes 27652
  438.3 11.0 %copy-start.4 = (bf16[2304,1536]{0,1:T(8,128)(2,1)S(1)}, bf16[2304,1536]{0,1:T(8,128)(2,1)}, u32[]{:S(2)}) copy-start(bf16[2304,1536]{0,1:T(8,128)(2,1)} %convert_element_type.101) | copy-start | bytes 21233668
  438.3 11.0 %copy-start.5 = (bf16[2304,512]{1,0:T(8,128)(2,1)S(1)}, bf16[2304,512]{1,0:T(8,128)(2,1)}, u32[]{:S(2)}) copy-start(bf16[2304,512]{1,0:T(8,128)(2,1)} %convert_element_type.104) | copy-start | bytes 7077892
  474.3 85.1 %collective-permute-start.1 = (bf16[2,48,6,512]{3,0,2,1:T(2,128)(2,1)}, bf16[2,48,6,512]{3,0,2,1:T(2,128)(2,1)}, u32[]{:S(2)}, u32[]{:S(2)}) collective-permute-start(bf16[2,48,6,512]{3,0,2,1:T(2,128)(2,1)} %slice.33), channel_id=1, source_target_pairs={{0,8},{8,16},{16,24},{24,32},{32,40},{40,48},{48,56},{56,64},{64,7... | collective-permute-start | bytes 1769480 | tf_op jit(solution)/shard_map/ppermute | solution.py:16
  626.6 3.9 copy-start.6
  626.7 4.8 copy-start.8
Sparse Core Ops, SparseCore 0:
  11.0 57.3 all-gather.1
  455.0 171.5 all-reduce.4
where the time goes:
time: 645 us; the launch traced here: 639 us
  local copies, waits for them, and re-layouts  170 us (26%)
  matrix products  142 us (22%)
  blocking collectives  135 us (21%)
  other arithmetic  97.8 us (15%)
  waiting for transfers between devices  61.4 us (10%)
  starting transfers between devices  17.2 us (3%)
  between operations  15.3 us (2%)
    dot_general x6, matrix products, prod(): return jnp.einsum(form, left, right, preferred_element_type=jnp.float32)  103 us
    psum x1, blocking collectives, body(): lax.psum((g_qkv, g_out, g_dec, g_gain), ('lat', 'lon'))  68.2 us
    psum x1, waiting for transfers between devices, body(): lax.psum((g_qkv, g_out, g_dec, g_gain), ('lat', 'lon'))  61.4 us
    scatter-add x1, other arithmetic, body(): grad_tok = jnp.zeros((tokens, outputs), jnp.float32).at[slot_cell.reshape...  48.8 us
    unnamed x52, local copies, waits for them, and re-layouts  36 us
    convert_element_type x2, local copies, waits for them, and re-layouts, attend_backward(): jnp.stack([dquery, dkey, dvalue], 2).astype(jnp.bfloat16)  30 us
    all_gather x1, blocking collectives, body(): all_weights = lax.all_gather(slot_weight, 'lat', axis=0, tiled=True)  28.9 us
    all_gather x1, blocking collectives, body(): lax.all_gather(slot_point, 'lat', axis=0, tiled=True)  28.1 us
  transfers between devices with their start and end apart: 4, of which 1 were waited for; matrix products, arithmetic and copies ran while one was open for 30% of the time, Pallas kernels for 0%

commit v1 on v0

v1 whole, which is shorter than its diff:
```python
import jax
import jax.numpy as jnp
from jax import lax
from jax.experimental import pallas as pl
from jax.experimental.pallas import tpu as pltpu
from jax.sharding import PartitionSpec as P

D = 512
HEADS = 8
HD = 64
WA = 6
WO = 12
WT = 144
C = 80
TOK = 2304
CAP = 512
BANDS = 8
PTS = 1024
SCALE = 0.125
F32 = jnp.float32
BF16 = jnp.bfloat16
NT = (((1,), (1,)), ((), ()))
TN = (((0,), (0,)), ((), ()))


def mm(a, b):
    return jnp.dot(a, b, preferred_element_type=F32)


def dg(a, b, dims):
    return lax.dot_general(a, b, dims, preferred_element_type=F32)


def onehot(idx_row, count):
    rows = lax.broadcasted_iota(jnp.int32, (count, idx_row.shape[1]), 0)
    return jnp.where(rows == idx_row, 1.0, 0.0).astype(BF16)


MESH = pl.DeviceIdType.MESH


def spot():
    return lax.axis_index("lat"), lax.axis_index("lon")


def device(lat, lon):
    return {"lat": lat, "lon": lon}


def greet(devices):
    barrier = pltpu.get_barrier_semaphore()
    for dev in devices:
        pl.semaphore_signal(barrier, inc=1, device_id=dev, device_id_type=MESH)
    pl.semaphore_wait(barrier, len(devices))


def remote(src, dst, send, recv, dev):
    return pltpu.make_async_remote_copy(
        src_ref=src, dst_ref=dst, send_sem=send, recv_sem=recv, device_id=dev, device_id_type=MESH
    )


def sub_iota(shape):
    return lax.broadcasted_iota(jnp.int32, shape, 1)


def norm_scale(x):
    return lax.rsqrt(jnp.mean(x * x, -1, keepdims=True) + 1e-06)


def steps_of(value, width, count):
    total = jnp.zeros_like(value)
    for n in range(1, count):
        total += jnp.where(value >= n * width, 1, 0)
    return total


def own_rows(cell):
    win = steps_of(cell, WT, 16)
    t = cell - win * WT
    r = steps_of(t, WO, 12)
    lo = t - r * WO
    low = r >= WA
    turn = jnp.where(low, 4, 0)
    mixed = 96 + (r - jnp.where(low, WA, 0)) * 8

    def wrap(v):
        return jnp.where(v >= 8, v - 8, v)

    a_row = jnp.where(
        (lo >= 2) & (lo < 10), r * 8 + lo - 2,
        mixed + wrap(jnp.where(lo < 2, lo + 6, lo - 10) + turn),
    )
    b_row = jnp.where(
        lo < 6, r * 8 + lo + 2,
        jnp.where(lo < 8, r * 8 + lo - 6, mixed + wrap(lo - 6 + turn)),
    )
    half = steps_of(win, 2, 8)
    second = win - half * 2
    return second * HALF + half * WT + jnp.where(second == 0, a_row, b_row)


NB = 8
HALF = NB * WT
NG = 4
GW = NG * HD
QC = 3 * GW
ER = 640


def start(copies):
    for copy in copies:
        copy.start()
    return copies


def finish(copies):
    for copy in copies:
        copy.wait()


def total_of(buf, n):
    acc = buf[0].astype(F32)
    for i in range(1, n):
        acc = acc + buf[i].astype(F32)
    return acc.astype(BF16)


class Sum:
    def __init__(self, src, out, rows, lanes, split_lanes, bufs, sems):
        self.src, self.out = src, out
        self.buf_a, self.sum_b, self.buf_b, self.sum_c, self.buf_c = bufs
        self.sems = sems
        lat, lon = spot()
        self.lat, self.lon = lat, lon
        self.core, self.grp = lax.rem(lon, 2), lax.div(lon, 2)
        self.sib = lon + 1 - 2 * self.core
        self.rows, self.lanes, self.split_lanes = rows, lanes, split_lanes
        self.half, self.band = lanes // 2, rows // 8
        self.grps = [lax.rem(self.grp + s, 8) for s in range(1, 8)]
        self.lats = [lax.rem(lat + s, 8) for s in range(1, 8)]
        self.step_no = 0

    def lane(self, core):
        return pl.ds(pl.multiple_of(core * self.half, 128), self.half)

    def rows_of(self, grp):
        return pl.ds(pl.multiple_of(grp * self.band, 16), self.band)

    def piece(self, lat):
        if self.split_lanes:
            n = self.half // 2
            return pl.ds(0, self.band), pl.ds(pl.multiple_of(lax.rem(lat, 2) * n, 128), n)
        n = self.band // 4
        return pl.ds(pl.multiple_of(lax.rem(lat, 4) * n, 16), n), pl.ds(0, self.half)

    def whole_piece(self, lat):
        if self.split_lanes:
            n = self.half // 2
            at = self.core * self.half + lax.rem(lat, 2) * n
            return self.rows_of(self.grp), pl.ds(pl.multiple_of(at, 128), n)
        n = self.band // 4
        at = self.grp * self.band + lax.rem(lat, 4) * n
        return pl.ds(pl.multiple_of(at, 16), n), self.lane(self.core)

    def copy(self, src, dst, n, dev):
        return remote(src, dst, self.sems.at[0, n], self.sems.at[1, n], dev)

    def step(self):
        getattr(self, "step%d" % self.step_no)()
        self.step_no += 1

    def step0(self):
        src = self.src.at[:, self.lane(1 - self.core)]
        self.flying = start([self.copy(src, self.buf_a, 0, device(self.lat, self.sib))])

    def step1(self):
        finish(self.flying)
        self.sum_b[...] = (
            self.src[:, self.lane(self.core)].astype(F32) + self.buf_a[...].astype(F32)
        ).astype(BF16)
        self.flying = start([
            self.copy(
                self.sum_b.at[self.rows_of(g)], self.buf_b.at[self.grp], 1 + s,
                device(self.lat, g * 2 + self.core),
            )
            for s, g in enumerate(self.grps)
        ])
        self.buf_b[self.grp] = self.sum_b[self.rows_of(self.grp)]

    def step2(self):
        finish(self.flying)
        self.sum_c[...] = total_of(self.buf_b, 8)
        self.flying = start([
            self.copy(
                self.sum_c.at[self.piece(o)], self.buf_c.at[self.lat], 8 + s, device(o, self.lon)
            )
            for s, o in enumerate(self.lats)
        ])
        self.buf_c[self.lat] = self.sum_c[self.piece(self.lat)]

    def step3(self):
        finish(self.flying)
        here = self.whole_piece(self.lat)
        self.out[here] = total_of(self.buf_c, 8)
        own = self.out.at[here]
        count = 2 if self.split_lanes else 4
        first = self.lat - lax.rem(self.lat, count)
        peers = [first + lax.rem(self.lat + s, count) for s in range(1, count)]
        self.flying = start([
            self.copy(own, own, 15 + s, device(o, self.lon)) for s, o in enumerate(peers)
        ])

    def step4(self):
        finish(self.flying)
        own = self.out.at[self.rows_of(self.grp), self.lane(self.core)]
        self.flying = start([
            self.copy(own, own, 18 + s, device(self.lat, g * 2 + self.core))
            for s, g in enumerate(self.grps)
        ])

    def step5(self):
        finish(self.flying)
        own = self.out.at[:, self.lane(self.core)]
        self.flying = start([self.copy(own, own, 25, device(self.lat, self.sib))])

    def step6(self):
        finish(self.flying)


def fused_kernel(
    x_hbm, pts_ref, slot_ref, weight_ref, count_ref, cell_ref, gain_ref, wqkv_hbm, wout_hbm,
    wdec_ref,
    gx_hbm, arrive_ref, qa_ref, qb_ref, e_ref,
    xv, wqkv, wout, load_sem, store_sem,
    sent, arr, asend, arecv, first, halo, edge, hsems,
    xw, nw, qkv, probs, att, oh, marr, gtt, dhf, dhb, datt, hid,
    src_a, src_b, src_e,
    a0, a1, a2, a3, a4, b0, b1, b2, b3, b4, e0, e1, e2, e3, e4, sems_a, sems_b, sems_e,
):
    lat, lon = spot()
    core, grp = lax.rem(lon, 2), lax.div(lon, 2)
    west, east = lax.rem(lon + 15, 16), lax.rem(lon + 1, 16)
    others = [lax.rem(lat + s, BANDS) for s in range(1, BANDS)]
    loads = start([
        pltpu.make_async_copy(x_hbm, xv, load_sem.at[0]),
        pltpu.make_async_copy(wqkv_hbm, wqkv, load_sem.at[1]),
        pltpu.make_async_copy(wout_hbm, wout, load_sem.at[2]),
    ])
    barrier = pltpu.get_barrier_semaphore()
    peers = (
        [device(lat, lon + 1 - 2 * core)]
        + [device(lat, lax.rem(grp + s, 8) * 2 + core) for s in range(1, 8)]
        + [device(o, lon) for o in others]
        + [device(lat, west), device(lat, east)]
    )
    for dev in peers:
        pl.semaphore_signal(barrier, inc=1, device_id=dev, device_id_type=MESH)

    sum_a = Sum(src_a, qa_ref, D, QC, False, (a0, a1, a2, a3, a4), sems_a)
    sum_b = Sum(src_b, qb_ref, D, QC, False, (b0, b1, b2, b3, b4), sems_b)
    sum_e = Sum(src_e, e_ref, ER, D, True, (e0, e1, e2, e3, e4), sems_e)

    pts = jnp.concatenate([pts_ref[:, n * 256 : (n + 1) * 256] for n in range(4)], axis=0)
    lane = lax.broadcasted_iota(jnp.int32, (1, CAP), 1)

    def rows_for(d):
        point = slot_ref[pl.ds(d, 1), :]
        quarter = steps_of(point, 256, 4)
        picked = mm(pts, onehot(point - quarter * 256, 256))
        rows = picked[0:C]
        for n in range(1, 4):
            rows = jnp.where(quarter == n, picked[n * C : (n + 1) * C], rows)
        live = lane < count_ref[pl.ds(d, 1), :]
        return jnp.where(live, weight_ref[pl.ds(d, 1), :] * rows, 0.0).astype(BF16)

    for s, o in enumerate(others):
        sent[s] = rows_for(o)
    arr[lat] = rows_for(lat)
    loads[0].wait()

    @pl.loop(0, NB)
    def _(lb):
        for lev in range(2):
            rows = pl.ds(pl.multiple_of(lb * 96 + lev * 48, 16), 48)
            part = xv[lev, pl.ds(lb * WA, WA)].astype(F32)[:, 0:8]
            first[rows, :] = part.reshape(48, D).astype(BF16)

    pl.semaphore_wait(barrier, len(peers))
    in_copy = remote(first, halo, hsems.at[0], hsems.at[1], device(lat, west))
    in_copy.start()
    copies = start([
        remote(sent.at[s], arr.at[lat], asend.at[s], arecv.at[s], device(o, lon))
        for s, o in enumerate(others)
    ])

    gain = gain_ref[...]

    def put_window(rows, toks):
        xw[rows, :] = toks.astype(BF16)
        nw[rows, :] = (toks * norm_scale(toks) * gain).astype(BF16)

    def project(at):
        @pl.loop(0, 6)
        def _(c):
            cols = pl.ds(pl.multiple_of(c * 256, 256), 256)
            qkv[at : at + HALF, cols] = mm(nw[at : at + HALF, :], wqkv[:, cols]).astype(BF16)

    @pl.loop(0, NB)
    def _(lb):
        x0 = xv[0, pl.ds(lb * WA, WA)].astype(F32)
        x1 = xv[1, pl.ds(lb * WA, WA)].astype(F32)
        sub = sub_iota((WA, 8, D))
        c0 = jnp.where(sub >= 6, x0[:, 0:8], x0[:, 16:24])
        c1 = jnp.where(sub >= 6, x1[:, 0:8], x1[:, 16:24])
        mixed = jnp.where((sub < 2) | (sub >= 6), c0, pltpu.roll(c1, 4, 1))
        toks = jnp.concatenate([x0[:, 8:16], x1[:, 8:16], mixed], axis=0).reshape(WT, D)
        put_window(pl.ds(pl.multiple_of(lb * WT, WT), WT), toks)

    loads[1].wait()
    project(0)

    head = lax.broadcasted_iota(jnp.int32, (1, GW), 1) // HD
    masks = [jnp.where(head == a, 1.0, 0.0).astype(BF16) for a in range(NG)]
    picks = [head == a for a in range(NG)]

    def stack(a):
        return jnp.concatenate([a * m for m in masks], axis=0)

    def pick(o):
        out = o[0:WT]
        for a in range(1, NG):
            out = jnp.where(picks[a], o[a * WT : (a + 1) * WT], out)
        return out

    def forward(w):
        rows = pl.ds(pl.multiple_of(w * WT, WT), WT)
        for g in range(HEADS // NG):
            cols = slice(g * GW, (g + 1) * GW)
            k = qkv[rows, D + g * GW : D + (g + 1) * GW]
            v = qkv[rows, 2 * D + g * GW : 2 * D + (g + 1) * GW]
            st = dg(k, stack(qkv[rows, cols] * BF16(SCALE)), NT)
            e = jnp.exp(st - jnp.max(st, axis=0, keepdims=True))
            pb = (e * (1.0 / jnp.sum(e, axis=0, keepdims=True))).astype(BF16)
            probs[g, rows, :] = pb
            att[rows, cols] = pick(dg(pb, v, TN)).astype(BF16)

    @pl.loop(0, NB)
    def _(w):
        forward(w)

    in_copy.wait()

    @pl.loop(0, NB)
    def _(lb):
        at = pl.multiple_of(lb * 96, 16)
        h0 = halo[pl.ds(at, 48), :].astype(F32).reshape(WA, 8, D)
        h1 = halo[pl.ds(pl.multiple_of(at + 48, 16), 48), :].astype(F32).reshape(WA, 8, D)
        x0 = xv[0, pl.ds(lb * WA, WA)].astype(F32)
        x1 = xv[1, pl.ds(lb * WA, WA)].astype(F32)
        sub = sub_iota((WA, 8, D))
        w0 = jnp.where(sub < 2, h0, x0[:, 16:24])
        w1 = jnp.where(sub < 2, h1, x1[:, 16:24])
        mixed = jnp.where((sub < 2) | (sub >= 6), pltpu.roll(h1, 4, 1), h0)
        toks = jnp.concatenate([w0, w1, mixed], axis=0).reshape(WT, D)
        put_window(pl.ds(pl.multiple_of(HALF + lb * WT, WT), WT), toks)

    project(HALF)

    @pl.loop(NB, 2 * NB)
    def _(w):
        forward(w)

    row = own_rows(cell_ref[...])
    block = steps_of(row, 256, 9)
    place = row - block * 256
    for i in range(BANDS):
        oh[:, i * CAP : (i + 1) * CAP] = onehot(place[i : i + 1, :], 256)
    finish(copies)
    for i in range(BANDS):
        part = arr[i]
        for b in range(9):
            mask = jnp.where(block[i : i + 1, :] == b, 1.0, 0.0).astype(BF16)
            marr[b * C : (b + 1) * C, i * CAP : (i + 1) * CAP] = part * mask
    toks = dg(marr[...], oh[...], NT).astype(BF16)
    for b in range(9):
        gtt[:, b * 256 : (b + 1) * 256] = toks[b * C : (b + 1) * C]
    loads[2].wait()

    @pl.loop(0, 9)
    def _(b):
        rows = pl.ds(pl.multiple_of(b * 256, 256), 256)
        dh = dg(gtt[:, rows], wdec_ref[...], TN)
        dhf[rows, :] = dh
        dhb[rows, :] = dh.astype(BF16)
        datt[rows, :] = dg(dh.astype(BF16), wout[...], NT).astype(BF16)
        hid[rows, :] = (xw[rows, :].astype(F32) + mm(att[rows, :], wout[...])).astype(BF16)

    src_e[0:D, :] = dg(att[...], dhb[...], TN).astype(BF16)
    src_e[D : D + C, :] = mm(gtt[...], hid[...]).astype(BF16)
    src_e[D + C : ER, :] = jnp.zeros((ER - D - C, D), BF16)
    sum_e.step()

    def backward(w, g):
        rows = pl.ds(pl.multiple_of(w * WT, WT), WT)
        cols = slice(g * GW, (g + 1) * GW)
        kcols = slice(D + g * GW, D + (g + 1) * GW)
        vcols = slice(2 * D + g * GW, 2 * D + (g + 1) * GW)
        k = qkv[rows, kcols]
        v = qkv[rows, vcols]
        qs = stack(qkv[rows, cols] * BF16(SCALE))
        ds = stack(datt[rows, cols])
        pb = probs[g, rows, :]
        p = pb.astype(F32)
        dp = dg(v, ds, NT)
        t = jnp.sum(p * dp, axis=0, keepdims=True)
        dst = (p * (dp - t)).astype(BF16)
        dv = mm(pb, ds)
        dk = mm(dst, qs)
        dq = pick(dg(dst, k, TN)) * SCALE
        qkv[rows, cols] = dq.astype(BF16)
        qkv[rows, kcols] = dk.astype(BF16)
        qkv[rows, vcols] = dv.astype(BF16)

    def back_loop(lo, hi, g):
        @pl.loop(lo, hi)
        def _(w):
            backward(w, g)

    def weight_grad(src, g):
        for n in range(3):
            part = dg(nw[...], qkv[:, n * D + g * GW : n * D + (g + 1) * GW], TN)
            src[:, n * GW : (n + 1) * GW] = part.astype(BF16)

    back_loop(0, NB, 0)
    sum_e.step()
    back_loop(NB, 2 * NB, 0)
    sum_e.step()
    weight_grad(src_a, 0)
    sum_a.step()
    back_loop(0, NB, 1)
    sum_e.step()
    sum_a.step()
    back_loop(NB, 2 * NB, 1)
    sum_e.step()
    sum_a.step()
    weight_grad(src_b, 1)
    sum_b.step()
    sum_e.step()
    sum_a.step()

    sub = sub_iota((WA, 8, D))

    def input_grad(lb):
        ys = []
        for s in range(2):
            rows = pl.ds(pl.multiple_of(s * HALF + lb * WT, WT), WT)
            x = xw[rows, :].astype(F32)
            dn = dg(qkv[rows, :], wqkv[...], NT)
            r = norm_scale(x)
            dng = dn * gain
            mean = jnp.mean(dng * x, -1, keepdims=True)
            y = dhf[rows, :] + r * (dng - x * (r * r * mean))
            ys.append(y.reshape(18, 8, D))
        ya, yb = ys
        m0, n0 = ya[12:18], yb[12:18]
        m1, n1 = pltpu.roll(m0, 4, 1), pltpu.roll(n0, 4, 1)
        at = pl.ds(lb * WA, WA)
        xv[0, at] = jnp.concatenate([m0, ya[0:6], jnp.where(sub < 2, m0, yb[0:6])], 1).astype(BF16)
        xv[1, at] = jnp.concatenate([m1, ya[6:12], jnp.where(sub < 2, m1, yb[6:12])], 1).astype(BF16)
        g0 = jnp.where(sub < 2, yb[0:6], n0).reshape(48, D)
        g1 = jnp.where(sub < 2, yb[6:12], n1).reshape(48, D)
        here = pl.multiple_of(lb * 96, 16)
        edge[pl.ds(here, 48), :] = g0.astype(BF16)
        edge[pl.ds(pl.multiple_of(here + 48, 16), 48), :] = g1.astype(BF16)

    outs = []

    def input_loop(n, lo, hi):
        @pl.loop(lo, hi)
        def _(lb):
            input_grad(lb)

        rows = pl.ds(lo * 96, (hi - lo) * 96)
        outs.append(remote(
            edge.at[rows], arrive_ref.at[rows], hsems.at[2 + 2 * n], hsems.at[3 + 2 * n],
            device(lat, east),
        ))
        outs[-1].start()
        at = pl.ds(lo * WA, (hi - lo) * WA)
        outs.append(pltpu.make_async_copy(xv.at[:, at], gx_hbm.at[:, at], store_sem.at[n]))
        outs[-1].start()

    input_loop(0, 0, 2)
    sum_b.step()
    sum_a.step()
    sum_e.step()
    input_loop(1, 2, 5)
    sum_b.step()
    sum_a.step()
    input_loop(2, 5, 8)
    sum_b.step()
    sum_a.step()
    sum_b.step()
    sum_b.step()
    sum_b.step()
    finish(outs)


def place_kernel(
    gx_ref, arrive_ref, qa_ref, qb_ref, e_ref, wqkv_ref, gain_ref,
    out_ref, gqkv_ref, gout_ref, gdec_ref, ggain_ref,
):
    sub = sub_iota((WA, 8, D))
    for lb in range(NB):
        for lev in range(2):
            at = slice(lb * WA, (lb + 1) * WA)
            x = gx_ref[lev, at].astype(F32)
            new = arrive_ref[lb * 96 + lev * 48 : lb * 96 + lev * 48 + 48].astype(F32)
            edge = jnp.where(sub < 6, new.reshape(WA, 8, D), x[:, 0:8])
            out_ref[lev, at] = jnp.concatenate([edge, x[:, 8:24]], 1).astype(BF16)
    acc = jnp.zeros((D, 128), F32)
    for g, q_ref in enumerate((qa_ref, qb_ref)):
        for n in range(3):
            cols = slice(n * D + g * GW, n * D + (g + 1) * GW)
            part = q_ref[:, n * GW : (n + 1) * GW].astype(F32)
            gqkv_ref[:, cols] = part
            prod = part * wqkv_ref[:, cols].astype(F32)
            acc += prod[:, 0:128] + prod[:, 128:256]
    ggain_ref[...] = jnp.sum(acc.T, axis=0, keepdims=True) / gain_ref[...]
    gout_ref[...] = e_ref[0:D].astype(F32)
    gdec_ref[...] = e_ref[D : D + C].astype(F32)


VM = pl.BlockSpec(memory_space=pltpu.VMEM)
ANY = pl.BlockSpec(memory_space=pl.ANY)
SDS = jax.ShapeDtypeStruct
DMA = pltpu.SemaphoreType.DMA


def sum_bufs(rows, lanes, split_lanes):
    half, band = lanes // 2, rows // 8
    piece = (band, half // 2) if split_lanes else (band // 4, half)
    shapes = [(rows, half), (rows, half), (8, band, half), (band, half), (8,) + piece]
    return [pltpu.VMEM(s, BF16) for s in shapes]


def fused_call(x, pts_t, slots, weights, counts, cells, gain, w_qkv, w_out, w_dec_t):
    def vm(*shape, dtype=BF16):
        return pltpu.VMEM(shape, dtype)

    return pl.pallas_call(
        fused_kernel,
        out_shape=(
            SDS(x.shape, BF16), SDS((768, D), BF16), SDS((D, QC), BF16), SDS((D, QC), BF16),
            SDS((ER, D), BF16),
        ),
        in_specs=[ANY] + [VM] * 6 + [ANY, ANY, VM],
        out_specs=(ANY, VM, VM, VM, VM),
        scratch_shapes=[
            vm(2, 48, 24, D), vm(D, 3 * D), vm(D, D), DMA((3,)), DMA((3,)),
            vm(7, C, CAP), vm(BANDS, C, CAP), DMA((7,)), DMA((7,)),
            vm(768, D), vm(768, D), vm(768, D), DMA((8,)),
            vm(TOK, D), vm(TOK, D), vm(TOK, 3 * D), vm(2, TOK, NG * WT), vm(TOK, D),
            vm(256, BANDS * CAP), vm(9 * C, BANDS * CAP), vm(C, TOK), vm(TOK, D, dtype=F32),
            vm(TOK, D), vm(TOK, D), vm(TOK, D),
            vm(D, QC), vm(D, QC), vm(ER, D),
            *sum_bufs(D, QC, False), *sum_bufs(D, QC, False), *sum_bufs(ER, D, True),
            DMA((2, 26)), DMA((2, 26)), DMA((2, 26)),
        ],
        compiler_params=pltpu.CompilerParams(
            vmem_limit_bytes=62 << 20, collective_id=0, has_side_effects=True
        ),
        name="fused",
    )(x, pts_t, slots, weights, counts, cells, gain, w_qkv, w_out, w_dec_t)


def place_call(gx, arriving, qa, qb, e, w_qkv, gain):
    return pl.pallas_call(
        place_kernel,
        out_shape=(
            SDS(gx.shape, BF16), SDS((D, 3 * D), F32), SDS((D, D), F32), SDS((C, D), F32),
            SDS((1, D), F32),
        ),
        in_specs=[VM] * 7,
        out_specs=(VM,) * 5,
        compiler_params=pltpu.CompilerParams(vmem_limit_bytes=40 << 20),
        name="place",
    )(gx, arriving, qa, qb, e, w_qkv, gain)


def body(
    block_input, gain, w_qkv, w_out, w_dec, g_points, slot_point, slot_cell, slot_weight, pair_count
):
    counts = jnp.broadcast_to(pair_count[:, None], slot_point.shape)
    parts = fused_call(
        block_input, g_points.T, slot_point, slot_weight, counts, slot_cell, gain[None],
        w_qkv, w_out, w_dec.T,
    )
    grad_x, g_qkv, g_out, g_dec, g_gain = place_call(*parts, w_qkv, gain[None])
    return (grad_x, g_qkv, g_out, g_dec.T, g_gain[0])


def solution(mesh):
    placed = (
        P(None, "lat", "lon", None),
        P(),
        P(),
        P(),
        P(),
        P(("lat", "lon"), None),
        P(("lat", "lon"), None),
        P(("lat", "lon"), None),
        P(("lat", "lon"), None),
        P(("lat", "lon")),
    )
    return jax.shard_map(
        body,
        mesh=mesh,
        in_specs=placed,
        out_specs=(P(None, "lat", "lon", None), P(), P(), P(), P()),
        check_vma=False,
    )
```

time: 645 us -> 120 us (0.19)
  local copies, waits for them, and re-layouts: 170 us -> 7.48 us
  matrix products: 142 us -> 0 us
  blocking collectives: 135 us -> 0 us
  Pallas kernels: 0 us -> 112 us
  other arithmetic: 97.8 us -> 0 us
  waiting for transfers between devices: 61.4 us -> 0 us
  starting transfers between devices: 17.2 us -> 0 us
  between operations: 15.3 us -> 0.67 us
    dot_general x13 -> x0, matrix products: 142 us -> none  [the longest x6 103 us: prod(): return jnp.einsum(form, left, right, preferred_element_type=jnp.float32)]
    pallas_call x0 -> x2, Pallas kernels: none -> 112 us  [the longest x1 109 us: fused_call(): pl.pallas_call(fused_kernel, out_shape=(SDS(x.shape, BF16), SDS((768, D),...]
    psum x1 -> x0, blocking collectives: 68.2 us -> none  [body(): lax.psum((g_qkv, g_out, g_dec, g_gain), ('lat', 'lon'))]
    psum x1 -> x0, waiting for transfers between devices: 61.4 us -> none  [body(): lax.psum((g_qkv, g_out, g_dec, g_gain), ('lat', 'lon'))]
    convert_element_type x8 -> x0, local copies, waits for them, and re-layouts: 59.7 us -> none  [the longest x2 30 us: attend_backward(): jnp.stack([dquery, dkey, dvalue], 2).astype(jnp.bfloat16)]
    all_gather x2 -> x0, blocking collectives: 57 us -> none  [the longest x1 28.9 us: body(): all_weights = lax.all_gather(slot_weight, 'lat', axis=0, tiled=True)]
    scatter-add x1 -> x0, other arithmetic: 48.8 us -> none  [body(): grad_tok = jnp.zeros((tokens, outputs), jnp.float32).at[slot_cell.reshape...]
    reshape x5 -> x0, local copies, waits for them, and re-layouts: 41.3 us -> none  [the longest x1 18 us: attend_forward(): qkv = qkv.astype(jnp.bfloat16).reshape(count, window, 3, HEADS, HD)]
  transfers between devices with their start and end apart: 4 -> 0, of which waited for: 1 -> 0; matrix products, arithmetic and copies ran while one was open for 30% -> 0% of each run, Pallas kernels for 0% -> 0%
where the time goes in v1:
time: 120 us
  Pallas kernels  112 us (93%)
  local copies, waits for them, and re-layouts  7.48 us (6%)
    pallas_call x1, Pallas kernels, fused_call(): pl.pallas_call(fused_kernel, out_shape=(SDS(x.shape, BF16), SDS((768, D),...  109 us
    unnamed x14, local copies, waits for them, and re-layouts  6.15 us
    pallas_call x1, Pallas kernels, place_call(): pl.pallas_call(place_kernel, out_shape=(SDS(gx.shape, BF16), SDS((D, 3 *...  3.27 us

profile of v1, /device:TPU:1, one launch (start us, length us, event | category | flops | bytes accessed | tf_op | source)
XLA Modules:
  0.0 120.1 jit_solution(4232363872714117423)
XLA Ops:
  0.6 1.3 %broadcast_in_dim.4.count_ref = s32[8,512]{1,0:T(8,128)} broadcast(s32[8]{0:T(128)} %param.19), dimensions={0} | broadcast | bytes 16416 | tf_op jit(solution)/shard_map/broadcast_in_dim | solution.py:595
  2.0 0.0 copy-start
  2.0 0.0 copy-start.6
  2.0 108.7 %fused.1 = (bf16[2,48,24,512]{3,2,1,0:T(8,128)(2,1)}, bf16[768,512]{1,0:T(8,128)(2,1)}, bf16[512,768]{1,0:T(8,128)(2,1)}, bf16[512,768]{1,0:T(8,128)(2,1)}, bf16[640,512]{1,0:T(8,128)(2,1)}) custom-call(bf16[2,48,24,512]{3,2,1,0:T(8,128)(2,1)} %x_hbm.1, bf16[80,1024]{1,0:T(8,128)(2,1)} %bitcast.7, s32[8,512]{1,0:T(8,128)} %slot_ref.1, f32[8,512]{1,0:T(8,128)} %weight_ref.1, ...), custom_call_target="tpu_custom_call" | custom-call | tf_op jit(solution)/shard_map/fused/pallas_call | solution.py:552
  110.7 0.0 copy-done
  110.7 0.0 copy-done.6
  110.7 0.0 copy-start.1
  110.7 1.7 %copy-done.1 = bf16[2,48,24,512]{3,2,1,0:T(8,128)(2,1)S(1)} copy-done((bf16[2,48,24,512]{3,2,1,0:T(8,128)(2,1)S(1)}, bf16[2,48,24,512]{3,2,1,0:T(8,128)(2,1)}, u32[]{:S(2)}) %copy-start.1) | copy-done | bytes 2359320
  112.3 0.0 copy-start.2
  112.4 1.1 copy-done.2
  113.5 0.0 copy-start.3
  113.5 1.1 copy-done.3
  114.6 0.0 copy-start.4
  114.6 1.1 copy-done.4
  115.8 0.0 copy-start.5
  115.8 1.1 copy-done.5
  116.8 3.3 %place.1 = (bf16[2,48,24,512]{3,2,1,0:T(8,128)(2,1)}, f32[512,1536]{1,0:T(8,128)}, f32[512,512]{1,0:T(8,128)}, f32[80,512]{1,0:T(8,128)}, f32[1,512]{1,0:T(1,128)}) custom-call(bf16[2,48,24,512]{3,2,1,0:T(8,128)(2,1)S(1)} %copy-done.1, bf16[768,512]{1,0:T(8,128)(2,1)S(1)} %copy-done.2, bf16[512,768]{1,0:T(8,128)(2,1)S(1)} %copy-done.3, ...), custom_call_target="tpu_custom_call" | custom-call | tf_op jit(solution)/shard_map/place/pallas_call | solution.py:579
Async XLA Ops:
  2.0 108.7 %copy-start = (bf16[512,1536]{1,0:T(8,128)(2,1)S(1)}, bf16[512,1536]{1,0:T(8,128)(2,1)}, u32[]{:S(2)}) copy-start(bf16[512,1536]{1,0:T(8,128)(2,1)} %wqkv_ref.1) | copy-start | bytes 4718596
  2.0 108.7 %copy-start.6 = (f32[512]{0:T(512)S(1)}, f32[512]{0:T(512)}, u32[]{:S(2)}) copy-start(f32[512]{0:T(512)} %param.11) | copy-start | bytes 6148
  110.7 1.7 %copy-start.1 = (bf16[2,48,24,512]{3,2,1,0:T(8,128)(2,1)S(1)}, bf16[2,48,24,512]{3,2,1,0:T(8,128)(2,1)}, u32[]{:S(2)}) copy-start(bf16[2,48,24,512]{3,2,1,0:T(8,128)(2,1)} %get-tuple-element.15.gx_ref) | copy-start | bytes 7077892
  112.3 1.1 copy-start.2
  113.5 1.1 copy-start.3
  114.6 1.1 copy-start.4
  115.8 1.1 copy-start.5

commit v2 on v1

v2 whole, which is shorter than its diff:
```python
import jax
import jax.numpy as jnp
from jax import lax
from jax.experimental import pallas as pl
from jax.experimental.pallas import tpu as pltpu
from jax.sharding import PartitionSpec as P

D = 512
HEADS = 8
HD = 64
WA = 6
WO = 12
WT = 144
C = 80
TOK = 2304
CAP = 512
BANDS = 8
PTS = 1024
SCALE = 0.125
F32 = jnp.float32
BF16 = jnp.bfloat16
NT = (((1,), (1,)), ((), ()))
TN = (((0,), (0,)), ((), ()))


def mm(a, b):
    return jnp.dot(a, b, preferred_element_type=F32)


def dg(a, b, dims):
    return lax.dot_general(a, b, dims, preferred_element_type=F32)


def onehot(idx_row, count):
    rows = lax.broadcasted_iota(jnp.int32, (count, idx_row.shape[1]), 0)
    return jnp.where(rows == idx_row, 1.0, 0.0).astype(BF16)


MESH = pl.DeviceIdType.MESH


def spot():
    return lax.axis_index("lat"), lax.axis_index("lon")


def device(lat, lon):
    return {"lat": lat, "lon": lon}


def greet(devices):
    barrier = pltpu.get_barrier_semaphore()
    for dev in devices:
        pl.semaphore_signal(barrier, inc=1, device_id=dev, device_id_type=MESH)
    pl.semaphore_wait(barrier, len(devices))


def remote(src, dst, send, recv, dev):
    return pltpu.make_async_remote_copy(
        src_ref=src, dst_ref=dst, send_sem=send, recv_sem=recv, device_id=dev, device_id_type=MESH
    )


def sub_iota(shape):
    return lax.broadcasted_iota(jnp.int32, shape, 1)


def norm_scale(x):
    return lax.rsqrt(jnp.mean(x * x, -1, keepdims=True) + 1e-06)


def steps_of(value, width, count):
    total = jnp.zeros_like(value)
    for n in range(1, count):
        total += jnp.where(value >= n * width, 1, 0)
    return total


def own_rows(cell):
    win = steps_of(cell, WT, 16)
    t = cell - win * WT
    r = steps_of(t, WO, 12)
    lo = t - r * WO
    low = r >= WA
    turn = jnp.where(low, 4, 0)
    mixed = 96 + (r - jnp.where(low, WA, 0)) * 8

    def wrap(v):
        return jnp.where(v >= 8, v - 8, v)

    a_row = jnp.where(
        (lo >= 2) & (lo < 10), r * 8 + lo - 2,
        mixed + wrap(jnp.where(lo < 2, lo + 6, lo - 10) + turn),
    )
    b_row = jnp.where(
        lo < 6, r * 8 + lo + 2,
        jnp.where(lo < 8, r * 8 + lo - 6, mixed + wrap(lo - 6 + turn)),
    )
    half = steps_of(win, 2, 8)
    second = win - half * 2
    return second * HALF + half * WT + jnp.where(second == 0, a_row, b_row)


NB = 8
HALF = NB * WT
GROUPS = ((0, 4), (4, 2), (6, 2))
ER = 640


def start(copies):
    for copy in copies:
        copy.start()
    return copies


def finish(copies):
    for copy in copies:
        copy.wait()


def total_of(buf, n):
    acc = buf[0].astype(F32)
    for i in range(1, n):
        acc = acc + buf[i].astype(F32)
    return acc.astype(BF16)


class Sum:
    def __init__(self, src, out, plan, bufs, sems):
        self.src, self.out = src, out
        self.buf_a, self.sum_b, self.buf_b, self.sum_c, self.buf_c = bufs
        self.sems = sems
        lat, lon = spot()
        self.lat, self.lon = lat, lon
        self.core, grp = lax.rem(lon, 2), lax.div(lon, 2)
        self.sib = lon + 1 - 2 * self.core
        self.rows, self.lanes, self.by_lanes, self.rp, self.lp, self.lat_first = plan
        self.hr = self.rows if self.by_lanes else self.rows // 2
        self.hl = self.lanes // 2 if self.by_lanes else self.lanes
        self.band = self.hr // 8
        self.pr, self.pl = self.band // self.rp, self.hl // self.lp
        self.one, self.two = (lat, grp) if self.lat_first else (grp, lat)
        self.step_no = 0

    def dev_one(self, n):
        if self.lat_first:
            return device(n, self.lon)
        return device(self.lat, n * 2 + self.core)

    def dev_two(self, n):
        if self.lat_first:
            return device(self.lat, n * 2 + self.core)
        return device(n, self.lon)

    def half(self, core):
        if self.by_lanes:
            return pl.ds(0, self.hr), pl.ds(pl.multiple_of(core * self.hl, 128), self.hl)
        return pl.ds(pl.multiple_of(core * self.hr, 16), self.hr), pl.ds(0, self.hl)

    def band_of(self, n):
        return pl.ds(pl.multiple_of(n * self.band, 16), self.band)

    def piece(self, n, row=0, lane=0):
        part = lax.rem(n, self.rp * self.lp)
        row = row + lax.rem(part, self.rp) * self.pr
        lane = lane + lax.div(part, self.rp) * self.pl
        return (
            pl.ds(pl.multiple_of(row, 16), self.pr), pl.ds(pl.multiple_of(lane, 128), self.pl)
        )

    def corner(self):
        row, lane = self.one * self.band, 0
        if self.by_lanes:
            lane = self.core * self.hl
        else:
            row = row + self.core * self.hr
        return row, lane

    def copy(self, src, dst, n, dev):
        return remote(src, dst, self.sems.at[0, n], self.sems.at[1, n], dev)

    def step(self):
        getattr(self, "step%d" % self.step_no)()
        self.step_no += 1

    def step0(self):
        src = self.src.at[self.half(1 - self.core)]
        self.flying = start([self.copy(src, self.buf_a, 0, device(self.lat, self.sib))])

    def step1(self):
        finish(self.flying)
        self.sum_b[...] = (
            self.src[self.half(self.core)].astype(F32) + self.buf_a[...].astype(F32)
        ).astype(BF16)
        self.flying = start([
            self.copy(
                self.sum_b.at[self.band_of(lax.rem(self.one + s, 8))], self.buf_b.at[self.one], s,
                self.dev_one(lax.rem(self.one + s, 8)),
            )
            for s in range(1, 8)
        ])
        self.buf_b[self.one] = self.sum_b[self.band_of(self.one)]

    def step2(self):
        finish(self.flying)
        self.sum_c[...] = total_of(self.buf_b, 8)
        self.flying = start([
            self.copy(
                self.sum_c.at[self.piece(lax.rem(self.two + s, 8))], self.buf_c.at[self.two],
                7 + s, self.dev_two(lax.rem(self.two + s, 8)),
            )
            for s in range(1, 8)
        ])
        self.buf_c[self.two] = self.sum_c[self.piece(self.two)]

    def step3(self):
        finish(self.flying)
        here = self.piece(self.two, *self.corner())
        self.out[here] = total_of(self.buf_c, 8)
        own = self.out.at[here]
        count = self.rp * self.lp
        first = self.two - lax.rem(self.two, count)
        self.flying = start([
            self.copy(own, own, 14 + s, self.dev_two(first + lax.rem(self.two + s, count)))
            for s in range(1, count)
        ])

    def step4(self):
        finish(self.flying)
        row, lane = self.corner()
        own = self.out.at[
            pl.ds(pl.multiple_of(row, 16), self.band), pl.ds(pl.multiple_of(lane, 128), self.hl)
        ]
        self.flying = start([
            self.copy(own, own, 17 + s, self.dev_one(lax.rem(self.one + s, 8)))
            for s in range(1, 8)
        ])

    def step5(self):
        finish(self.flying)
        own = self.out.at[self.half(self.core)]
        self.flying = start([self.copy(own, own, 25, device(self.lat, self.sib))])

    def step6(self):
        finish(self.flying)


PLAN_E = (ER, D, True, 1, 2, True)
PLAN_4 = (D, 768, True, 4, 1, False)
PLAN_2 = (D, 384, False, 2, 1, False)


def fused_kernel(
    x_hbm, pts_ref, slot_ref, weight_ref, count_ref, cell_ref, gain_ref, wqkv_hbm, wout_hbm,
    wdec_ref,
    gx_hbm, arrive_ref, qa_ref, qb_ref, qc_ref, e_ref,
    xv, wqkv, wout, load_sem, store_sem,
    sent, arr, asend, arecv, first, halo, edge, hsems,
    xw, nw, qkv, probs_a, probs_b, probs_c, att, oh, marr, gtt, dhf, dhb, datt, hid, dnf,
    src_a, src_b, src_c, src_e,
    a0, a1, a2, a3, a4, b0, b1, b2, b3, b4, c0, c1, c2, c3, c4, e0, e1, e2, e3, e4,
    sems_a, sems_b, sems_c, sems_e,
):
    lat, lon = spot()
    core, grp = lax.rem(lon, 2), lax.div(lon, 2)
    west, east = lax.rem(lon + 15, 16), lax.rem(lon + 1, 16)
    others = [lax.rem(lat + s, BANDS) for s in range(1, BANDS)]
    loads = start([
        pltpu.make_async_copy(x_hbm, xv, load_sem.at[0]),
        pltpu.make_async_copy(wqkv_hbm, wqkv, load_sem.at[1]),
        pltpu.make_async_copy(wout_hbm, wout, load_sem.at[2]),
    ])
    barrier = pltpu.get_barrier_semaphore()
    peers = (
        [device(lat, lon + 1 - 2 * core)]
        + [device(lat, lax.rem(grp + s, 8) * 2 + core) for s in range(1, 8)]
        + [device(o, lon) for o in others]
        + [device(lat, west), device(lat, east)]
    )
    for dev in peers:
        pl.semaphore_signal(barrier, inc=1, device_id=dev, device_id_type=MESH)

    sum_a = Sum(src_a, qa_ref, PLAN_4, (a0, a1, a2, a3, a4), sems_a)
    sum_b = Sum(src_b, qb_ref, PLAN_2, (b0, b1, b2, b3, b4), sems_b)
    sum_c = Sum(src_c, qc_ref, PLAN_2, (c0, c1, c2, c3, c4), sems_c)
    sum_e = Sum(src_e, e_ref, PLAN_E, (e0, e1, e2, e3, e4), sems_e)
    probs = (probs_a, probs_b, probs_c)

    pts = jnp.concatenate([pts_ref[:, n * 256 : (n + 1) * 256] for n in range(4)], axis=0)
    lane = lax.broadcasted_iota(jnp.int32, (1, CAP), 1)

    def rows_for(d):
        point = slot_ref[pl.ds(d, 1), :]
        quarter = steps_of(point, 256, 4)
        picked = mm(pts, onehot(point - quarter * 256, 256))
        rows = picked[0:C]
        for n in range(1, 4):
            rows = jnp.where(quarter == n, picked[n * C : (n + 1) * C], rows)
        live = lane < count_ref[d]
        return jnp.where(live, weight_ref[pl.ds(d, 1), :] * rows, 0.0).astype(BF16)

    for s, o in enumerate(others):
        sent[s] = rows_for(o)
    arr[lat] = rows_for(lat)
    loads[0].wait()

    @pl.loop(0, NB)
    def _(lb):
        for lev in range(2):
            rows = pl.ds(pl.multiple_of(lb * 96 + lev * 48, 16), 48)
            part = xv[lev, pl.ds(lb * WA, WA)].astype(F32)[:, 0:8]
            first[rows, :] = part.reshape(48, D).astype(BF16)

    pl.semaphore_wait(barrier, len(peers))
    in_copy = remote(first, halo, hsems.at[0], hsems.at[1], device(lat, west))
    in_copy.start()
    copies = start([
        remote(sent.at[s], arr.at[lat], asend.at[s], arecv.at[s], device(o, lon))
        for s, o in enumerate(others)
    ])

    gain = gain_ref[...]

    def put_window(rows, toks):
        xw[rows, :] = toks.astype(BF16)
        nw[rows, :] = (toks * norm_scale(toks) * gain).astype(BF16)

    def project(at):
        @pl.loop(0, 6)
        def _(c):
            cols = pl.ds(pl.multiple_of(c * 256, 256), 256)
            qkv[at : at + HALF, cols] = mm(nw[at : at + HALF, :], wqkv[:, cols]).astype(BF16)

    @pl.loop(0, NB)
    def _(lb):
        x0 = xv[0, pl.ds(lb * WA, WA)].astype(F32)
        x1 = xv[1, pl.ds(lb * WA, WA)].astype(F32)
        sub = sub_iota((WA, 8, D))
        c0 = jnp.where(sub >= 6, x0[:, 0:8], x0[:, 16:24])
        c1 = jnp.where(sub >= 6, x1[:, 0:8], x1[:, 16:24])
        mixed = jnp.where((sub < 2) | (sub >= 6), c0, pltpu.roll(c1, 4, 1))
        toks = jnp.concatenate([x0[:, 8:16], x1[:, 8:16], mixed], axis=0).reshape(WT, D)
        put_window(pl.ds(pl.multiple_of(lb * WT, WT), WT), toks)

    loads[1].wait()
    project(0)

    masks, picks = {}, {}
    for n in (4, 2):
        head = lax.broadcasted_iota(jnp.int32, (1, n * HD), 1) // HD
        masks[n] = [jnp.where(head == a, 1.0, 0.0).astype(BF16) for a in range(n)]
        picks[n] = [head == a for a in range(n)]

    def stack(a, n):
        return jnp.concatenate([a * m for m in masks[n]], axis=0)

    def pick(o, n):
        out = o[0:WT]
        for a in range(1, n):
            out = jnp.where(picks[n][a], o[a * WT : (a + 1) * WT], out)
        return out

    def col(part, g):
        at, n = GROUPS[g]
        return slice(part * D + at * HD, part * D + (at + n) * HD)

    def window(w):
        return pl.ds(pl.multiple_of(w * WT, WT), WT)

    def forward(w):
        for some in ((0,), (1, 2)):
            todo = [(window(2 * w + i), g) for i in range(2) for g in some]
            scores = [
                dg(qkv[rows, col(1, g)], stack(qkv[rows, col(0, g)] * BF16(SCALE), GROUPS[g][1]), NT)
                for rows, g in todo
            ]
            pbs = []
            for st in scores:
                e = jnp.exp(st - jnp.max(st, axis=0, keepdims=True))
                pbs.append((e * (1.0 / jnp.sum(e, axis=0, keepdims=True))).astype(BF16))
            outs = [dg(pb, qkv[rows, col(2, g)], TN) for pb, (rows, g) in zip(pbs, todo)]
            for pb, o, (rows, g) in zip(pbs, outs, todo):
                probs[g][rows, :] = pb
                att[rows, col(0, g)] = pick(o, GROUPS[g][1]).astype(BF16)

    @pl.loop(0, NB // 2)
    def _(w):
        forward(w)

    in_copy.wait()

    @pl.loop(0, NB)
    def _(lb):
        at = pl.multiple_of(lb * 96, 16)
        h0 = halo[pl.ds(at, 48), :].astype(F32).reshape(WA, 8, D)
        h1 = halo[pl.ds(pl.multiple_of(at + 48, 16), 48), :].astype(F32).reshape(WA, 8, D)
        x0 = xv[0, pl.ds(lb * WA, WA)].astype(F32)
        x1 = xv[1, pl.ds(lb * WA, WA)].astype(F32)
        sub = sub_iota((WA, 8, D))
        w0 = jnp.where(sub < 2, h0, x0[:, 16:24])
        w1 = jnp.where(sub < 2, h1, x1[:, 16:24])
        mixed = jnp.where((sub < 2) | (sub >= 6), pltpu.roll(h1, 4, 1), h0)
        toks = jnp.concatenate([w0, w1, mixed], axis=0).reshape(WT, D)
        put_window(pl.ds(pl.multiple_of(HALF + lb * WT, WT), WT), toks)

    project(HALF)

    @pl.loop(NB // 2, NB)
    def _(w):
        forward(w)

    row = own_rows(cell_ref[...])
    block = steps_of(row, 256, 9)
    place = row - block * 256
    for i in range(BANDS):
        oh[:, i * CAP : (i + 1) * CAP] = onehot(place[i : i + 1, :], 256)
    finish(copies)
    for i in range(BANDS):
        part = arr[i]
        for b in range(9):
            mask = jnp.where(block[i : i + 1, :] == b, 1.0, 0.0).astype(BF16)
            marr[b * C : (b + 1) * C, i * CAP : (i + 1) * CAP] = part * mask
    toks = dg(marr[...], oh[...], NT).astype(BF16)
    for b in range(9):
        gtt[:, b * 256 : (b + 1) * 256] = toks[b * C : (b + 1) * C]
    loads[2].wait()

    @pl.loop(0, 3)
    def _(b):
        rows = pl.ds(pl.multiple_of(b * 768, 768), 768)
        dh = dg(gtt[:, rows], wdec_ref[...], TN)
        dhf[rows, :] = dh
        dhb[rows, :] = dh.astype(BF16)
        datt[rows, :] = dg(dh.astype(BF16), wout[...], NT).astype(BF16)
        hid[rows, :] = (xw[rows, :].astype(F32) + mm(att[rows, :], wout[...])).astype(BF16)

    src_e[0:D, :] = dg(att[...], dhb[...], TN).astype(BF16)
    src_e[D : D + C, :] = mm(gtt[...], hid[...]).astype(BF16)
    src_e[D + C : ER, :] = jnp.zeros((ER - D - C, D), BF16)
    sum_e.step()

    def backward(w, g):
        n = GROUPS[g][1]
        todo = [window(2 * w + i) for i in range(2)]
        ks = [qkv[rows, col(1, g)] for rows in todo]
        qs = [stack(qkv[rows, col(0, g)] * BF16(SCALE), n) for rows in todo]
        ds = [stack(datt[rows, col(0, g)], n) for rows in todo]
        pbs = [probs[g][rows, :] for rows in todo]
        dps = [dg(qkv[rows, col(2, g)], d, NT) for rows, d in zip(todo, ds)]
        dvs = [mm(pb, d) for pb, d in zip(pbs, ds)]
        dsts = []
        for pb, dp in zip(pbs, dps):
            p = pb.astype(F32)
            t = jnp.sum(p * dp, axis=0, keepdims=True)
            dsts.append((p * (dp - t)).astype(BF16))
        dks = [mm(dst, q) for dst, q in zip(dsts, qs)]
        dqs = [pick(dg(dst, k, TN), n) * SCALE for dst, k in zip(dsts, ks)]
        for rows, dq, dk, dv in zip(todo, dqs, dks, dvs):
            qkv[rows, col(0, g)] = dq.astype(BF16)
            qkv[rows, col(1, g)] = dk.astype(BF16)
            qkv[rows, col(2, g)] = dv.astype(BF16)

    def back_loop(lo, hi, g):
        @pl.loop(lo // 2, hi // 2)
        def _(w):
            backward(w, g)

    def weight_grad(src, g):
        width = GROUPS[g][1] * HD
        for n in range(3):
            part = dg(nw[...], qkv[:, col(n, g)], TN)
            src[:, n * width : (n + 1) * width] = part.astype(BF16)

    back_loop(0, 4, 0)
    sum_e.step()
    back_loop(4, 16, 0)
    sum_e.step()
    weight_grad(src_a, 0)
    sum_a.step()
    back_loop(0, 8, 1)
    sum_e.step()
    sum_a.step()
    back_loop(8, 16, 1)
    sum_e.step()
    weight_grad(src_b, 1)
    sum_b.step()
    back_loop(0, 8, 2)
    sum_a.step()
    sum_b.step()
    back_loop(8, 16, 2)
    sum_a.step()
    weight_grad(src_c, 2)
    sum_c.step()
    sum_e.step()
    sum_a.step()
    sum_b.step()

    sub = sub_iota((WA, 8, D))

    def project_back(at):
        for n in range(2):
            cols = slice(n * 256, (n + 1) * 256)
            dnf[:, cols] = dg(qkv[at : at + HALF, :], wqkv[cols, :], NT)

    def input_grad(at, lb):
        rows = pl.ds(pl.multiple_of(at + lb * WT, WT), WT)
        x = xw[rows, :].astype(F32)
        r = norm_scale(x)
        dng = dnf[window(lb), :] * gain
        mean = jnp.mean(dng * x, -1, keepdims=True)
        y = dhf[rows, :] + r * (dng - x * (r * r * mean))
        return y.reshape(18, 8, D)

    outs = []

    def second_windows(lo, hi, n):
        @pl.loop(lo, hi)
        def _(lb):
            y = input_grad(HALF, lb)
            mix = y[12:18]
            turned = pltpu.roll(mix, 4, 1)
            at = pl.ds(lb * WA, WA)
            for lev, m in enumerate((mix, turned)):
                main = y[lev * 6 : lev * 6 + 6]
                xv[lev, at] = jnp.concatenate([main, main, main], 1).astype(BF16)
                here = pl.ds(pl.multiple_of(lb * 96 + lev * 48, 16), 48)
                edge[here, :] = jnp.where(sub < 2, main, m).reshape(48, D).astype(BF16)

        rows = pl.ds(lo * 96, (hi - lo) * 96)
        outs.append(remote(
            edge.at[rows], arrive_ref.at[rows], hsems.at[2 + 2 * n], hsems.at[3 + 2 * n],
            device(lat, east),
        ))
        outs[-1].start()

    def first_windows(lo, hi, n):
        @pl.loop(lo, hi)
        def _(lb):
            y = input_grad(0, lb)
            mix = y[12:18]
            turned = pltpu.roll(mix, 4, 1)
            at = pl.ds(lb * WA, WA)
            for lev, m in enumerate((mix, turned)):
                main = y[lev * 6 : lev * 6 + 6]
                right = jnp.where(sub < 2, m, xv[lev, at].astype(F32)[:, 16:24])
                xv[lev, at] = jnp.concatenate([m, main, right], 1).astype(BF16)

        at = pl.ds(lo * WA, (hi - lo) * WA)
        outs.append(pltpu.make_async_copy(xv.at[:, at], gx_hbm.at[:, at], store_sem.at[n]))
        outs[-1].start()

    project_back(HALF)
    sum_c.step()
    second_windows(0, 4, 0)
    sum_b.step()
    sum_e.step()
    second_windows(4, 8, 1)
    sum_c.step()
    sum_b.step()
    project_back(0)
    sum_a.step()
    sum_c.step()
    first_windows(0, 4, 0)
    sum_c.step()
    sum_b.step()
    first_windows(4, 8, 1)
    sum_a.step()
    sum_c.step()
    sum_b.step()
    sum_c.step()
    finish(outs)


def place_kernel(
    gx_ref, arrive_ref, qa_ref, qb_ref, qc_ref, e_ref, edec_ref, wqkv_ref, gain_ref,
    out_ref, gqkv_ref, gout_ref, gdec_ref, ggain_ref,
):
    sub = sub_iota((WA, 8, D))
    for lb in range(2):
        for lev in range(2):
            at = slice(lb * WA, (lb + 1) * WA)
            x = gx_ref[lev, at].astype(F32)
            new = arrive_ref[lb * 96 + lev * 48 : lb * 96 + lev * 48 + 48].astype(F32)
            edge = jnp.where(sub < 6, new.reshape(WA, 8, D), x[:, 0:8])
            out_ref[lev, at] = jnp.concatenate([edge, x[:, 8:24]], 1).astype(BF16)
    acc = jnp.zeros((128, 128), F32)
    for (first, count), q_ref in zip(GROUPS, (qa_ref, qb_ref, qc_ref)):
        width = count * HD
        for n in range(3):
            cols = slice(n * D + first * HD, n * D + first * HD + width)
            part = q_ref[:, n * width : (n + 1) * width].astype(F32)
            gqkv_ref[:, cols] = part
            prod = part * wqkv_ref[:, cols].astype(F32)
            for k in range(0, width, 128):
                acc += prod[:, k : k + 128]
    ggain_ref[...] = jnp.sum(acc.T, axis=0, keepdims=True) / gain_ref[...]
    gout_ref[...] = e_ref[...].astype(F32)
    gdec_ref[...] = edec_ref[0:C].astype(F32)


VM = pl.BlockSpec(memory_space=pltpu.VMEM)
ANY = pl.BlockSpec(memory_space=pl.ANY)
SDS = jax.ShapeDtypeStruct
DMA = pltpu.SemaphoreType.DMA


SM = pl.BlockSpec(memory_space=pltpu.SMEM)


def sum_bufs(plan):
    rows, lanes, by_lanes, rp, lp, _ = plan
    rows, lanes = (rows, lanes // 2) if by_lanes else (rows // 2, lanes)
    band = rows // 8
    shapes = [(rows, lanes), (rows, lanes), (8, band, lanes), (band, lanes)]
    shapes.append((8, band // rp, lanes // lp))
    return [pltpu.VMEM(s, BF16) for s in shapes]


def fused_call(x, pts_t, slots, weights, counts, cells, gain, w_qkv, w_out, w_dec_t):
    def vm(*shape, dtype=BF16):
        return pltpu.VMEM(shape, dtype)

    return pl.pallas_call(
        fused_kernel,
        out_shape=(
            SDS(x.shape, BF16), SDS((768, D), BF16), SDS((D, 768), BF16), SDS((D, 384), BF16),
            SDS((D, 384), BF16), SDS((ER, D), BF16),
        ),
        in_specs=[ANY, VM, VM, VM, SM, VM, VM, ANY, ANY, VM],
        out_specs=(ANY, VM, VM, VM, VM, VM),
        scratch_shapes=[
            vm(2, 48, 24, D), vm(D, 3 * D), vm(D, D), DMA((3,)), DMA((3,)),
            vm(7, C, CAP), vm(BANDS, C, CAP), DMA((7,)), DMA((7,)),
            vm(768, D), vm(768, D), vm(768, D), DMA((8,)),
            vm(TOK, D), vm(TOK, D), vm(TOK, 3 * D),
            vm(TOK, 4 * WT), vm(TOK, 2 * WT), vm(TOK, 2 * WT), vm(TOK, D),
            vm(256, BANDS * CAP), vm(9 * C, BANDS * CAP), vm(C, TOK), vm(TOK, D, dtype=F32),
            vm(TOK, D), vm(TOK, D), vm(TOK, D), vm(HALF, D, dtype=F32),
            vm(D, 768), vm(D, 384), vm(D, 384), vm(ER, D),
            *sum_bufs(PLAN_4), *sum_bufs(PLAN_2), *sum_bufs(PLAN_2), *sum_bufs(PLAN_E),
            DMA((2, 26)), DMA((2, 26)), DMA((2, 26)), DMA((2, 26)),
        ],
        compiler_params=pltpu.CompilerParams(
            vmem_limit_bytes=62 << 20, collective_id=0, has_side_effects=True
        ),
        name="fused",
    )(x, pts_t, slots, weights, counts, cells, gain, w_qkv, w_out, w_dec_t)


def place_call(gx, arriving, qa, qb, qc, e, w_qkv, gain):
    def rows(lanes):
        return pl.BlockSpec((128, lanes), lambda i: (i, 0))

    grid_rows = pl.BlockSpec((2, 12, 24, D), lambda i: (0, i, 0, 0))
    across = pl.BlockSpec((1, 128), lambda i: (0, i))
    return pl.pallas_call(
        place_kernel,
        grid=(4,),
        out_shape=(
            SDS(gx.shape, BF16), SDS((D, 3 * D), F32), SDS((D, D), F32), SDS((C, D), F32),
            SDS((1, D), F32),
        ),
        in_specs=[
            grid_rows, pl.BlockSpec((192, D), lambda i: (i, 0)), rows(768), rows(384), rows(384),
            rows(D), pl.BlockSpec((128, D), lambda i: (4, 0)), rows(3 * D), across,
        ],
        out_specs=(grid_rows, rows(3 * D), rows(D), pl.BlockSpec((C, D), lambda i: (0, 0)), across),
        compiler_params=pltpu.CompilerParams(vmem_limit_bytes=60 << 20),
        name="place",
    )(gx, arriving, qa, qb, qc, e, e, w_qkv, gain)


def body(
    block_input, gain, w_qkv, w_out, w_dec, g_points, slot_point, slot_cell, slot_weight, pair_count
):
    parts = fused_call(
        block_input, g_points.T, slot_point, slot_weight, pair_count, slot_cell, gain[None],
        w_qkv, w_out, w_dec.T,
    )
    grad_x, g_qkv, g_out, g_dec, g_gain = place_call(*parts, w_qkv, gain[None])
    return (grad_x, g_qkv, g_out, g_dec.T, g_gain[0])


def solution(mesh):
    placed = (
        P(None, "lat", "lon", None),
        P(),
        P(),
        P(),
        P(),
        P(("lat", "lon"), None),
        P(("lat", "lon"), None),
        P(("lat", "lon"), None),
        P(("lat", "lon"), None),
        P(("lat", "lon")),
    )
    return jax.shard_map(
        body,
        mesh=mesh,
        in_specs=placed,
        out_specs=(P(None, "lat", "lon", None), P(), P(), P(), P()),
        check_vma=False,
    )
```

time: 120 us -> 107 us (0.89)
  local copies, waits for them, and re-layouts: 7.48 us -> 0 us
  Pallas kernels: 112 us -> 106 us
    pallas_call x1, Pallas kernels: 109 us -> 99.7 us  [fused_call(): pl.pallas_call(fused_kernel, out_shape=(SDS(x.shape, BF16), SDS((768, D),...]
    unnamed x14 -> x0, local copies, waits for them, and re-layouts: 6.15 us -> none
    pallas_call x1, Pallas kernels: 3.27 us -> 6.48 us  [place_call(): pl.pallas_call(place_kernel, grid=(4,), out_shape=(SDS(gx.shape, BF16), S...]
    broadcast_in_dim x1 -> x0, local copies, waits for them, and re-layouts: 1.33 us -> none  [body(): counts = jnp.broadcast_to(pair_count[:, None], slot_point.shape)]
where the time goes in v2:
time: 107 us
  Pallas kernels  106 us (99%)
    pallas_call x1, Pallas kernels, fused_call(): pl.pallas_call(fused_kernel, out_shape=(SDS(x.shape, BF16), SDS((768, D),...  99.7 us
    pallas_call x1, Pallas kernels, place_call(): pl.pallas_call(place_kernel, grid=(4,), out_shape=(SDS(gx.shape, BF16), S...  6.48 us

profile of v2, /device:TPU:1, one launch (start us, length us, event | category | flops | bytes accessed | tf_op | source)
XLA Modules:
  0.0 107.0 jit_solution(10820988567051006638)
XLA Ops:
  0.6 99.7 %fused.1 = (bf16[2,48,24,512]{3,2,1,0:T(8,128)(2,1)}, bf16[768,512]{1,0:T(8,128)(2,1)}, bf16[512,768]{1,0:T(8,128)(2,1)}, bf16[512,384]{1,0:T(8,128)(2,1)}, bf16...) custom-call(bf16[2,48,24,512]{3,2,1,0:T(8,128)(2,1)} %x_hbm.1, bf16[80,1024]{1,0:T(8,128)(2,1)} %bitcast.5, ...), custom_call_target="tpu_custom_call" | custom-call | tf_op jit(solution)/shard_map/fused/pallas_call | solution.py:622
  100.4 6.5 %place.1 = (bf16[2,48,24,512]{3,2,1,0:T(8,128)(2,1)}, f32[512,1536]{1,0:T(8,128)}, f32[512,512]{1,0:T(8,128)}, f32[80,512]{1,0:T(8,128)}, f32[1,512]{1,0:T(1,128)}) custom-call(bf16[2,48,24,512]{3,2,1,0:T(8,128)(2,1)} %get-tuple-element.16.gx_ref, bf16[768,512]{1,0:T(8,128)(2,1)} %get-tuple-element.17.arrive_ref, bf16[512,768]{1,0:T(8,128)(2,1)} %get-tuple-element.18.qa_ref, ...), custom_call_target="tpu_custom_call" | custom-call | tf_op jit(solution)/shard_map/place/pallas_call | solution.py:655

commit v3 on v2

--- a/solution.py
+++ b/solution.py
@@ -366,25 +366,27 @@
     def window(w):
         return pl.ds(pl.multiple_of(w * WT, WT), WT)
 
-    def forward(w):
-        for some in ((0,), (1, 2)):
-            todo = [(window(2 * w + i), g) for i in range(2) for g in some]
-            scores = [
-                dg(qkv[rows, col(1, g)], stack(qkv[rows, col(0, g)] * BF16(SCALE), GROUPS[g][1]), NT)
-                for rows, g in todo
-            ]
-            pbs = []
-            for st in scores:
-                e = jnp.exp(st - jnp.max(st, axis=0, keepdims=True))
-                pbs.append((e * (1.0 / jnp.sum(e, axis=0, keepdims=True))).astype(BF16))
-            outs = [dg(pb, qkv[rows, col(2, g)], TN) for pb, (rows, g) in zip(pbs, todo)]
-            for pb, o, (rows, g) in zip(pbs, outs, todo):
-                probs[g][rows, :] = pb
-                att[rows, col(0, g)] = pick(o, GROUPS[g][1]).astype(BF16)
-
-    @pl.loop(0, NB // 2)
-    def _(w):
-        forward(w)
+    def forward(w, some):
+        todo = [(window(2 * w + i), g) for i in range(2) for g in some]
+        scores = [
+            dg(qkv[rows, col(1, g)], stack(qkv[rows, col(0, g)] * BF16(SCALE), GROUPS[g][1]), NT)
+            for rows, g in todo
+        ]
+        pbs = []
+        for st in scores:
+            e = jnp.exp(st - jnp.max(st, axis=0, keepdims=True))
+            pbs.append((e * (1.0 / jnp.sum(e, axis=0, keepdims=True))).astype(BF16))
+        outs = [dg(pb, qkv[rows, col(2, g)], TN) for pb, (rows, g) in zip(pbs, todo)]
+        for pb, o, (rows, g) in zip(pbs, outs, todo):
+            probs[g][rows, :] = pb
+            att[rows, col(0, g)] = pick(o, GROUPS[g][1]).astype(BF16)
+
+    def forward_loop(lo, hi, some):
+        @pl.loop(lo // 2, hi // 2)
+        def _(w):
+            forward(w, some)
+
+    forward_loop(0, NB, (0,))
 
     in_copy.wait()
 
@@ -404,9 +406,7 @@
 
     project(HALF)
 
-    @pl.loop(NB // 2, NB)
-    def _(w):
-        forward(w)
+    forward_loop(NB, 2 * NB, (0,))
 
     row = own_rows(cell_ref[...])
     block = steps_of(row, 256, 9)
@@ -431,12 +431,16 @@
         dhf[rows, :] = dh
         dhb[rows, :] = dh.astype(BF16)
         datt[rows, :] = dg(dh.astype(BF16), wout[...], NT).astype(BF16)
-        hid[rows, :] = (xw[rows, :].astype(F32) + mm(att[rows, :], wout[...])).astype(BF16)
-
-    src_e[0:D, :] = dg(att[...], dhb[...], TN).astype(BF16)
-    src_e[D : D + C, :] = mm(gtt[...], hid[...]).astype(BF16)
-    src_e[D + C : ER, :] = jnp.zeros((ER - D - C, D), BF16)
-    sum_e.step()
+
+    def hidden_grads():
+        @pl.loop(0, 3)
+        def _(b):
+            rows = pl.ds(pl.multiple_of(b * 768, 768), 768)
+            hid[rows, :] = (xw[rows, :].astype(F32) + mm(att[rows, :], wout[...])).astype(BF16)
+
+        src_e[0:D, :] = dg(att[...], dhb[...], TN).astype(BF16)
+        src_e[D : D + C, :] = mm(gtt[...], hid[...]).astype(BF16)
+        src_e[D + C : ER, :] = jnp.zeros((ER - D - C, D), BF16)
 
     def backward(w, g):
         n = GROUPS[g][1]
@@ -470,29 +474,27 @@
             part = dg(nw[...], qkv[:, col(n, g)], TN)
             src[:, n * width : (n + 1) * width] = part.astype(BF16)
 
-    back_loop(0, 4, 0)
-    sum_e.step()
-    back_loop(4, 16, 0)
-    sum_e.step()
+    back_loop(0, 16, 0)
     weight_grad(src_a, 0)
     sum_a.step()
-    back_loop(0, 8, 1)
+    forward_loop(0, 8, (1, 2))
+    sum_a.step()
+    forward_loop(8, 16, (1, 2))
+    hidden_grads()
     sum_e.step()
     sum_a.step()
-    back_loop(8, 16, 1)
+    back_loop(0, 16, 1)
     sum_e.step()
+    sum_a.step()
     weight_grad(src_b, 1)
     sum_b.step()
     back_loop(0, 8, 2)
     sum_a.step()
+    back_loop(8, 16, 2)
     sum_b.step()
-    back_loop(8, 16, 2)
-    sum_a.step()
     weight_grad(src_c, 2)
     sum_c.step()
     sum_e.step()
-    sum_a.step()
-    sum_b.step()
 
     sub = sub_iota((WA, 8, D))
 
@@ -549,40 +551,42 @@
         outs[-1].start()
 
     project_back(HALF)
+    second_windows(0, 4, 0)
     sum_c.step()
-    second_windows(0, 4, 0)
-    sum_b.step()
     sum_e.step()
+    sum_a.step()
     second_windows(4, 8, 1)
-    sum_c.step()
     sum_b.step()
     project_back(0)
+    sum_e.step()
     sum_a.step()
-    sum_c.step()
     first_windows(0, 4, 0)
-    sum_c.step()
     sum_b.step()
     first_windows(4, 8, 1)
-    sum_a.step()
     sum_c.step()
     sum_b.step()
     sum_c.step()
+    sum_e.step()
+    sum_c.step()
+    sum_b.step()
+    sum_c.step()
+    sum_e.step()
+    sum_b.step()
+    sum_c.step()
     finish(outs)
 
 
 def place_kernel(
     gx_ref, arrive_ref, qa_ref, qb_ref, qc_ref, e_ref, edec_ref, wqkv_ref, gain_ref,
-    out_ref, gqkv_ref, gout_ref, gdec_ref, ggain_ref,
+    out_ref, gqkv_ref, gout_ref, gdec_ref, ggain_ref, gains,
 ):
     sub = sub_iota((WA, 8, D))
-    for lb in range(2):
-        for lev in range(2):
-            at = slice(lb * WA, (lb + 1) * WA)
-            x = gx_ref[lev, at].astype(F32)
-            new = arrive_ref[lb * 96 + lev * 48 : lb * 96 + lev * 48 + 48].astype(F32)
-            edge = jnp.where(sub < 6, new.reshape(WA, 8, D), x[:, 0:8])
-            out_ref[lev, at] = jnp.concatenate([edge, x[:, 8:24]], 1).astype(BF16)
-    acc = jnp.zeros((128, 128), F32)
+    for lev in range(2):
+        x = gx_ref[lev].astype(F32)
+        new = arrive_ref[lev * 48 : lev * 48 + 48].astype(F32)
+        edge = jnp.where(sub < 6, new.reshape(WA, 8, D), x[:, 0:8])
+        out_ref[lev] = jnp.concatenate([edge, x[:, 8:24]], 1).astype(BF16)
+    acc = jnp.zeros((64, 128), F32)
     for (first, count), q_ref in zip(GROUPS, (qa_ref, qb_ref, qc_ref)):
         width = count * HD
         for n in range(3):
@@ -592,7 +596,13 @@
             prod = part * wqkv_ref[:, cols].astype(F32)
             for k in range(0, width, 128):
                 acc += prod[:, k : k + 128]
-    ggain_ref[...] = jnp.sum(acc.T, axis=0, keepdims=True) / gain_ref[...]
+    step = pl.program_id(0)
+    gains[pl.ds(pl.multiple_of(step * 64, 64), 64), :] = acc
+
+    @pl.when(step == 7)
+    def _():
+        ggain_ref[...] = jnp.sum(gains[...].T, axis=0, keepdims=True) / gain_ref[...]
+
     gout_ref[...] = e_ref[...].astype(F32)
     gdec_ref[...] = edec_ref[0:C].astype(F32)
 
@@ -648,22 +658,23 @@
 
 def place_call(gx, arriving, qa, qb, qc, e, w_qkv, gain):
     def rows(lanes):
-        return pl.BlockSpec((128, lanes), lambda i: (i, 0))
-
-    grid_rows = pl.BlockSpec((2, 12, 24, D), lambda i: (0, i, 0, 0))
-    across = pl.BlockSpec((1, 128), lambda i: (0, i))
+        return pl.BlockSpec((64, lanes), lambda i: (i, 0))
+
+    grid_rows = pl.BlockSpec((2, WA, 24, D), lambda i: (0, i, 0, 0))
+    across = pl.BlockSpec((1, D), lambda i: (0, 0))
     return pl.pallas_call(
         place_kernel,
-        grid=(4,),
+        grid=(8,),
         out_shape=(
             SDS(gx.shape, BF16), SDS((D, 3 * D), F32), SDS((D, D), F32), SDS((C, D), F32),
             SDS((1, D), F32),
         ),
         in_specs=[
-            grid_rows, pl.BlockSpec((192, D), lambda i: (i, 0)), rows(768), rows(384), rows(384),
+            grid_rows, pl.BlockSpec((96, D), lambda i: (i, 0)), rows(768), rows(384), rows(384),
             rows(D), pl.BlockSpec((128, D), lambda i: (4, 0)), rows(3 * D), across,
         ],
         out_specs=(grid_rows, rows(3 * D), rows(D), pl.BlockSpec((C, D), lambda i: (0, 0)), across),
+        scratch_shapes=[pltpu.VMEM((D, 128), F32)],
         compiler_params=pltpu.CompilerParams(vmem_limit_bytes=60 << 20),
         name="place",
     )(gx, arriving, qa, qb, qc, e, e, w_qkv, gain)

time: 107 us -> 115 us (1.075)
  Pallas kernels: 106 us -> 114 us
    pallas_call x1, Pallas kernels: 99.7 us -> 106 us  [fused_call(): pl.pallas_call(fused_kernel, out_shape=(SDS(x.shape, BF16), SDS((768, D),...]
    pallas_call x1, Pallas kernels: 6.48 us -> 8.34 us  [place_call(): pl.pallas_call(place_kernel, grid=(8,), out_shape=(SDS(gx.shape, BF16), S...]
where the time goes in v3:
time: 115 us
  Pallas kernels  114 us (99%)
    pallas_call x1, Pallas kernels, fused_call(): pl.pallas_call(fused_kernel, out_shape=(SDS(x.shape, BF16), SDS((768, D),...  106 us
    pallas_call x1, Pallas kernels, place_call(): pl.pallas_call(place_kernel, grid=(8,), out_shape=(SDS(gx.shape, BF16), S...  8.34 us

profile of v3, /device:TPU:1, one launch (start us, length us, event | category | flops | bytes accessed | tf_op | source)
XLA Modules:
  0.0 115.0 jit_solution(9130981626186600162)
XLA Ops:
  0.6 105.8 %fused.1 = (bf16[2,48,24,512]{3,2,1,0:T(8,128)(2,1)}, bf16[768,512]{1,0:T(8,128)(2,1)}, bf16[512,768]{1,0:T(8,128)(2,1)}, bf16[512,384]{1,0:T(8,128)(2,1)}, bf16...) custom-call(bf16[2,48,24,512]{3,2,1,0:T(8,128)(2,1)} %x_hbm.1, bf16[80,1024]{1,0:T(8,128)(2,1)} %bitcast.5, ...), custom_call_target="tpu_custom_call" | custom-call | tf_op jit(solution)/shard_map/fused/pallas_call | solution.py:632
  106.5 8.3 %place.1 = (bf16[2,48,24,512]{3,2,1,0:T(8,128)(2,1)}, f32[512,1536]{1,0:T(8,128)}, f32[512,512]{1,0:T(8,128)}, f32[80,512]{1,0:T(8,128)}, f32[1,512]{1,0:T(1,128)}) custom-call(bf16[2,48,24,512]{3,2,1,0:T(8,128)(2,1)} %get-tuple-element.16.gx_ref, bf16[768,512]{1,0:T(8,128)(2,1)} %get-tuple-element.17.arrive_ref, bf16[512,768]{1,0:T(8,128)(2,1)} %get-tuple-element.18.qa_ref, ...), custom_call_target="tpu_custom_call" | custom-call | tf_op jit(solution)/shard_map/place/pallas_call | solution.py:665

commit v4 on v3

--- a/solution.py
+++ b/solution.py
@@ -127,29 +127,39 @@
 class Sum:
     def __init__(self, src, out, plan, bufs, sems):
         self.src, self.out = src, out
-        self.buf_a, self.sum_b, self.buf_b, self.sum_c, self.buf_c = bufs
+        self.buf_a, self.sum_b, self.buf_b, self.sum_c, self.buf_c, self.buf_d = bufs
         self.sems = sems
         lat, lon = spot()
         self.lat, self.lon = lat, lon
-        self.core, grp = lax.rem(lon, 2), lax.div(lon, 2)
+        self.core = lax.rem(lon, 2)
+        self.z, self.y = lax.div(lon, 4), lax.rem(lat, 4)
+        self.xlo, self.xhi = lax.rem(lax.div(lon, 2), 2), lax.div(lat, 4)
+        self.x = self.xhi * 2 + self.xlo
         self.sib = lon + 1 - 2 * self.core
-        self.rows, self.lanes, self.by_lanes, self.rp, self.lp, self.lat_first = plan
+        self.rows, self.lanes, self.by_lanes, self.rp, self.lp, self.y_first = plan
         self.hr = self.rows if self.by_lanes else self.rows // 2
         self.hl = self.lanes // 2 if self.by_lanes else self.lanes
-        self.band = self.hr // 8
+        self.band = self.hr // 4
         self.pr, self.pl = self.band // self.rp, self.hl // self.lp
-        self.one, self.two = (lat, grp) if self.lat_first else (grp, lat)
+        self.one, self.two = (self.y, self.z) if self.y_first else (self.z, self.y)
         self.step_no = 0
 
+    def at_z(self, n):
+        return device(self.lat, n * 4 + lax.rem(self.lon, 4))
+
+    def at_y(self, n):
+        return device(self.xhi * 4 + n, self.lon)
+
+    def at_x(self, n):
+        return device(
+            lax.div(n, 2) * 4 + self.y, self.z * 4 + lax.rem(n, 2) * 2 + self.core
+        )
+
     def dev_one(self, n):
-        if self.lat_first:
-            return device(n, self.lon)
-        return device(self.lat, n * 2 + self.core)
+        return self.at_y(n) if self.y_first else self.at_z(n)
 
     def dev_two(self, n):
-        if self.lat_first:
-            return device(self.lat, n * 2 + self.core)
-        return device(n, self.lon)
+        return self.at_z(n) if self.y_first else self.at_y(n)
 
     def half(self, core):
         if self.by_lanes:
@@ -160,9 +170,8 @@
         return pl.ds(pl.multiple_of(n * self.band, 16), self.band)
 
     def piece(self, n, row=0, lane=0):
-        part = lax.rem(n, self.rp * self.lp)
-        row = row + lax.rem(part, self.rp) * self.pr
-        lane = lane + lax.div(part, self.rp) * self.pl
+        row = row + lax.rem(n, self.rp) * self.pr
+        lane = lane + lax.div(n, self.rp) * self.pl
         return (
             pl.ds(pl.multiple_of(row, 16), self.pr), pl.ds(pl.multiple_of(lane, 128), self.pl)
         )
@@ -191,62 +200,65 @@
         self.sum_b[...] = (
             self.src[self.half(self.core)].astype(F32) + self.buf_a[...].astype(F32)
         ).astype(BF16)
+        peers = [lax.rem(self.one + s, 4) for s in range(1, 4)]
         self.flying = start([
-            self.copy(
-                self.sum_b.at[self.band_of(lax.rem(self.one + s, 8))], self.buf_b.at[self.one], s,
-                self.dev_one(lax.rem(self.one + s, 8)),
-            )
-            for s in range(1, 8)
+            self.copy(self.sum_b.at[self.band_of(o)], self.buf_b.at[self.one], 1 + s, self.dev_one(o))
+            for s, o in enumerate(peers)
         ])
         self.buf_b[self.one] = self.sum_b[self.band_of(self.one)]
 
     def step2(self):
         finish(self.flying)
-        self.sum_c[...] = total_of(self.buf_b, 8)
+        self.sum_c[...] = total_of(self.buf_b, 4)
+        peers = [lax.rem(self.two + s, 4) for s in range(1, 4)]
         self.flying = start([
-            self.copy(
-                self.sum_c.at[self.piece(lax.rem(self.two + s, 8))], self.buf_c.at[self.two],
-                7 + s, self.dev_two(lax.rem(self.two + s, 8)),
-            )
-            for s in range(1, 8)
+            self.copy(self.sum_c.at[self.piece(o)], self.buf_c.at[self.two], 4 + s, self.dev_two(o))
+            for s, o in enumerate(peers)
         ])
         self.buf_c[self.two] = self.sum_c[self.piece(self.two)]
 
     def step3(self):
         finish(self.flying)
+        self.buf_d[self.x] = total_of(self.buf_c, 4)
+        own = self.buf_d.at[self.x]
+        self.flying = start([
+            self.copy(own, own, 7 + s, self.at_x(lax.rem(self.x + 1 + s, 4))) for s in range(3)
+        ])
+
+    def step4(self):
+        finish(self.flying)
         here = self.piece(self.two, *self.corner())
-        self.out[here] = total_of(self.buf_c, 8)
+        self.out[here] = total_of(self.buf_d, 4)
         own = self.out.at[here]
-        count = self.rp * self.lp
-        first = self.two - lax.rem(self.two, count)
         self.flying = start([
-            self.copy(own, own, 14 + s, self.dev_two(first + lax.rem(self.two + s, count)))
-            for s in range(1, count)
+            self.copy(own, own, 10 + s, self.dev_two(lax.rem(self.two + 1 + s, 4)))
+            for s in range(3)
         ])
 
-    def step4(self):
+    def step5(self):
         finish(self.flying)
         row, lane = self.corner()
         own = self.out.at[
             pl.ds(pl.multiple_of(row, 16), self.band), pl.ds(pl.multiple_of(lane, 128), self.hl)
         ]
         self.flying = start([
-            self.copy(own, own, 17 + s, self.dev_one(lax.rem(self.one + s, 8)))
-            for s in range(1, 8)
+            self.copy(own, own, 13 + s, self.dev_one(lax.rem(self.one + 1 + s, 4)))
+            for s in range(3)
         ])
 
-    def step5(self):
+    def step6(self):
         finish(self.flying)
         own = self.out.at[self.half(self.core)]
-        self.flying = start([self.copy(own, own, 25, device(self.lat, self.sib))])
-
-    def step6(self):
+        self.flying = start([self.copy(own, own, 16, device(self.lat, self.sib))])
+
+    def step7(self):
         finish(self.flying)
 
 
-PLAN_E = (ER, D, True, 1, 2, True)
+PLAN_E = (ER, D, True, 2, 2, True)
 PLAN_4 = (D, 768, True, 4, 1, False)
-PLAN_2 = (D, 384, False, 2, 1, False)
+PLAN_2 = (D, 384, False, 4, 1, False)
+PLAN_2Y = (D, 384, False, 4, 1, True)
 
 
 def fused_kernel(
@@ -257,11 +269,12 @@
     sent, arr, asend, arecv, first, halo, edge, hsems,
     xw, nw, qkv, probs_a, probs_b, probs_c, att, oh, marr, gtt, dhf, dhb, datt, hid, dnf,
     src_a, src_b, src_c, src_e,
-    a0, a1, a2, a3, a4, b0, b1, b2, b3, b4, c0, c1, c2, c3, c4, e0, e1, e2, e3, e4,
+    a0, a1, a2, a3, a4, a5, b0, b1, b2, b3, b4, b5, c0, c1, c2, c3, c4, c5, e0, e1, e2, e3, e4, e5,
     sems_a, sems_b, sems_c, sems_e,
 ):
     lat, lon = spot()
-    core, grp = lax.rem(lon, 2), lax.div(lon, 2)
+    core = lax.rem(lon, 2)
+    flip = lon + 2 - 4 * lax.rem(lax.div(lon, 2), 2)
     west, east = lax.rem(lon + 15, 16), lax.rem(lon + 1, 16)
     others = [lax.rem(lat + s, BANDS) for s in range(1, BANDS)]
     loads = start([
@@ -272,17 +285,18 @@
     barrier = pltpu.get_barrier_semaphore()
     peers = (
         [device(lat, lon + 1 - 2 * core)]
-        + [device(lat, lax.rem(grp + s, 8) * 2 + core) for s in range(1, 8)]
+        + [device(lat, lax.rem(lon + 4 * s, 16)) for s in range(1, 4)]
+        + [device(o, flip) for o in (lat, lax.rem(lat + 4, BANDS))]
         + [device(o, lon) for o in others]
         + [device(lat, west), device(lat, east)]
     )
     for dev in peers:
         pl.semaphore_signal(barrier, inc=1, device_id=dev, device_id_type=MESH)
 
-    sum_a = Sum(src_a, qa_ref, PLAN_4, (a0, a1, a2, a3, a4), sems_a)
-    sum_b = Sum(src_b, qb_ref, PLAN_2, (b0, b1, b2, b3, b4), sems_b)
-    sum_c = Sum(src_c, qc_ref, PLAN_2, (c0, c1, c2, c3, c4), sems_c)
-    sum_e = Sum(src_e, e_ref, PLAN_E, (e0, e1, e2, e3, e4), sems_e)
+    sum_a = Sum(src_a, qa_ref, PLAN_4, (a0, a1, a2, a3, a4, a5), sems_a)
+    sum_b = Sum(src_b, qb_ref, PLAN_2, (b0, b1, b2, b3, b4, b5), sems_b)
+    sum_c = Sum(src_c, qc_ref, PLAN_2Y, (c0, c1, c2, c3, c4, c5), sems_c)
+    sum_e = Sum(src_e, e_ref, PLAN_E, (e0, e1, e2, e3, e4, e5), sems_e)
     probs = (probs_a, probs_b, probs_c)
 
     pts = jnp.concatenate([pts_ref[:, n * 256 : (n + 1) * 256] for n in range(4)], axis=0)
@@ -298,9 +312,6 @@
         live = lane < count_ref[d]
         return jnp.where(live, weight_ref[pl.ds(d, 1), :] * rows, 0.0).astype(BF16)
 
-    for s, o in enumerate(others):
-        sent[s] = rows_for(o)
-    arr[lat] = rows_for(lat)
     loads[0].wait()
 
     @pl.loop(0, NB)
@@ -313,10 +324,11 @@
     pl.semaphore_wait(barrier, len(peers))
     in_copy = remote(first, halo, hsems.at[0], hsems.at[1], device(lat, west))
     in_copy.start()
-    copies = start([
-        remote(sent.at[s], arr.at[lat], asend.at[s], arecv.at[s], device(o, lon))
-        for s, o in enumerate(others)
-    ])
+    copies = []
+    for s, o in enumerate(others):
+        sent[s] = rows_for(o)
+        copies += start([remote(sent.at[s], arr.at[lat], asend.at[s], arecv.at[s], device(o, lon))])
+    arr[lat] = rows_for(lat)
 
     gain = gain_ref[...]
 
@@ -387,7 +399,7 @@
             forward(w, some)
 
     forward_loop(0, NB, (0,))
-
+    forward_loop(0, NB, (1, 2))
     in_copy.wait()
 
     @pl.loop(0, NB)
@@ -477,24 +489,28 @@
     back_loop(0, 16, 0)
     weight_grad(src_a, 0)
     sum_a.step()
-    forward_loop(0, 8, (1, 2))
+    forward_loop(8, 16, (1, 2))
     sum_a.step()
-    forward_loop(8, 16, (1, 2))
     hidden_grads()
     sum_e.step()
+    back_loop(0, 8, 1)
     sum_a.step()
-    back_loop(0, 16, 1)
     sum_e.step()
+    back_loop(8, 16, 1)
     sum_a.step()
     weight_grad(src_b, 1)
     sum_b.step()
+    sum_e.step()
     back_loop(0, 8, 2)
     sum_a.step()
+    sum_b.step()
+    sum_e.step()
     back_loop(8, 16, 2)
-    sum_b.step()
+    sum_a.step()
+    sum_e.step()
     weight_grad(src_c, 2)
     sum_c.step()
-    sum_e.step()
+    sum_b.step()
 
     sub = sub_iota((WA, 8, D))
 
@@ -551,27 +567,27 @@
         outs[-1].start()
 
     project_back(HALF)
+    sum_a.step()
+    sum_b.step()
+    sum_e.step()
     second_windows(0, 4, 0)
     sum_c.step()
+    sum_b.step()
+    second_windows(4, 8, 1)
+    sum_c.step()
+    sum_b.step()
     sum_e.step()
-    sum_a.step()
-    second_windows(4, 8, 1)
+    project_back(0)
+    sum_c.step()
     sum_b.step()
-    project_back(0)
-    sum_e.step()
     sum_a.step()
     first_windows(0, 4, 0)
-    sum_b.step()
+    sum_c.step()
+    sum_e.step()
     first_windows(4, 8, 1)
     sum_c.step()
     sum_b.step()
     sum_c.step()
-    sum_e.step()
-    sum_c.step()
-    sum_b.step()
-    sum_c.step()
-    sum_e.step()
-    sum_b.step()
     sum_c.step()
     finish(outs)
 
@@ -581,12 +597,14 @@
     out_ref, gqkv_ref, gout_ref, gdec_ref, ggain_ref, gains,
 ):
     sub = sub_iota((WA, 8, D))
-    for lev in range(2):
-        x = gx_ref[lev].astype(F32)
-        new = arrive_ref[lev * 48 : lev * 48 + 48].astype(F32)
-        edge = jnp.where(sub < 6, new.reshape(WA, 8, D), x[:, 0:8])
-        out_ref[lev] = jnp.concatenate([edge, x[:, 8:24]], 1).astype(BF16)
-    acc = jnp.zeros((64, 128), F32)
+    for lb in range(2):
+        for lev in range(2):
+            at = slice(lb * WA, (lb + 1) * WA)
+            x = gx_ref[lev, at].astype(F32)
+            new = arrive_ref[lb * 96 + lev * 48 : lb * 96 + lev * 48 + 48].astype(F32)
+            edge = jnp.where(sub < 6, new.reshape(WA, 8, D), x[:, 0:8])
+            out_ref[lev, at] = jnp.concatenate([edge, x[:, 8:24]], 1).astype(BF16)
+    acc = jnp.zeros((128, 128), F32)
     for (first, count), q_ref in zip(GROUPS, (qa_ref, qb_ref, qc_ref)):
         width = count * HD
         for n in range(3):
@@ -597,9 +615,9 @@
             for k in range(0, width, 128):
                 acc += prod[:, k : k + 128]
     step = pl.program_id(0)
-    gains[pl.ds(pl.multiple_of(step * 64, 64), 64), :] = acc
-
-    @pl.when(step == 7)
+    gains[pl.ds(pl.multiple_of(step * 128, 128), 128), :] = acc
+
+    @pl.when(step == 3)
     def _():
         ggain_ref[...] = jnp.sum(gains[...].T, axis=0, keepdims=True) / gain_ref[...]
 
@@ -619,9 +637,9 @@
 def sum_bufs(plan):
     rows, lanes, by_lanes, rp, lp, _ = plan
     rows, lanes = (rows, lanes // 2) if by_lanes else (rows // 2, lanes)
-    band = rows // 8
-    shapes = [(rows, lanes), (rows, lanes), (8, band, lanes), (band, lanes)]
-    shapes.append((8, band // rp, lanes // lp))
+    band = rows // 4
+    shapes = [(rows, lanes), (rows, lanes), (4, band, lanes), (band, lanes)]
+    shapes += [(4, band // rp, lanes // lp)] * 2
     return [pltpu.VMEM(s, BF16) for s in shapes]
 
 
@@ -647,7 +665,7 @@
             vm(TOK, D), vm(TOK, D), vm(TOK, D), vm(HALF, D, dtype=F32),
             vm(D, 768), vm(D, 384), vm(D, 384), vm(ER, D),
             *sum_bufs(PLAN_4), *sum_bufs(PLAN_2), *sum_bufs(PLAN_2), *sum_bufs(PLAN_E),
-            DMA((2, 26)), DMA((2, 26)), DMA((2, 26)), DMA((2, 26)),
+            DMA((2, 17)), DMA((2, 17)), DMA((2, 17)), DMA((2, 17)),
         ],
         compiler_params=pltpu.CompilerParams(
             vmem_limit_bytes=62 << 20, collective_id=0, has_side_effects=True
@@ -658,19 +676,19 @@
 
 def place_call(gx, arriving, qa, qb, qc, e, w_qkv, gain):
     def rows(lanes):
-        return pl.BlockSpec((64, lanes), lambda i: (i, 0))
-
-    grid_rows = pl.BlockSpec((2, WA, 24, D), lambda i: (0, i, 0, 0))
+        return pl.BlockSpec((128, lanes), lambda i: (i, 0))
+
+    grid_rows = pl.BlockSpec((2, 12, 24, D), lambda i: (0, i, 0, 0))
     across = pl.BlockSpec((1, D), lambda i: (0, 0))
     return pl.pallas_call(
         place_kernel,
-        grid=(8,),
+        grid=(4,),
         out_shape=(
             SDS(gx.shape, BF16), SDS((D, 3 * D), F32), SDS((D, D), F32), SDS((C, D), F32),
             SDS((1, D), F32),
         ),
         in_specs=[
-            grid_rows, pl.BlockSpec((96, D), lambda i: (i, 0)), rows(768), rows(384), rows(384),
+            grid_rows, pl.BlockSpec((192, D), lambda i: (i, 0)), rows(768), rows(384), rows(384),
             rows(D), pl.BlockSpec((128, D), lambda i: (4, 0)), rows(3 * D), across,
         ],
         out_specs=(grid_rows, rows(3 * D), rows(D), pl.BlockSpec((C, D), lambda i: (0, 0)), across),

time: 115 us -> 110 us (0.957)
  Pallas kernels: 114 us -> 109 us
    pallas_call x1, Pallas kernels: 106 us -> 102 us  [fused_call(): pl.pallas_call(fused_kernel, out_shape=(SDS(x.shape, BF16), SDS((768, D),...]
    pallas_call x1, Pallas kernels: 8.34 us -> 6.39 us  [place_call(): pl.pallas_call(place_kernel, grid=(4,), out_shape=(SDS(gx.shape, BF16), S...]
where the time goes in v4:
time: 110 us; the launch traced here: 109 us
  Pallas kernels  109 us (99%)
    pallas_call x1, Pallas kernels, fused_call(): pl.pallas_call(fused_kernel, out_shape=(SDS(x.shape, BF16), SDS((768, D),...  102 us
    pallas_call x1, Pallas kernels, place_call(): pl.pallas_call(place_kernel, grid=(4,), out_shape=(SDS(gx.shape, BF16), S...  6.39 us

profile of v4, /device:TPU:1, one launch (start us, length us, event | category | flops | bytes accessed | tf_op | source)
XLA Modules:
  0.0 109.4 jit_solution(12199054992643142849)
XLA Ops:
  0.6 102.3 %fused.1 = (bf16[2,48,24,512]{3,2,1,0:T(8,128)(2,1)}, bf16[768,512]{1,0:T(8,128)(2,1)}, bf16[512,768]{1,0:T(8,128)(2,1)}, bf16[512,384]{1,0:T(8,128)(2,1)}, bf16...) custom-call(bf16[2,48,24,512]{3,2,1,0:T(8,128)(2,1)} %x_hbm.1, bf16[80,1024]{1,0:T(8,128)(2,1)} %bitcast.5, ...), custom_call_target="tpu_custom_call" | custom-call | tf_op jit(solution)/shard_map/fused/pallas_call | solution.py:650
  102.9 6.4 %place.1 = (bf16[2,48,24,512]{3,2,1,0:T(8,128)(2,1)}, f32[512,1536]{1,0:T(8,128)}, f32[512,512]{1,0:T(8,128)}, f32[80,512]{1,0:T(8,128)}, f32[1,512]{1,0:T(1,128)}) custom-call(bf16[2,48,24,512]{3,2,1,0:T(8,128)(2,1)} %get-tuple-element.16.gx_ref, bf16[768,512]{1,0:T(8,128)(2,1)} %get-tuple-element.17.arrive_ref, bf16[512,768]{1,0:T(8,128)(2,1)} %get-tuple-element.18.qa_ref, ...), custom_call_target="tpu_custom_call" | custom-call | tf_op jit(solution)/shard_map/place/pallas_call | solution.py:683

commit v5 on v4

--- a/solution.py
+++ b/solution.py
@@ -398,8 +398,8 @@
         def _(w):
             forward(w, some)
 
-    forward_loop(0, NB, (0,))
-    forward_loop(0, NB, (1, 2))
+    forward_loop(0, 8, (0,))
+    forward_loop(0, 8, (1, 2))
     in_copy.wait()
 
     @pl.loop(0, NB)
@@ -418,7 +418,8 @@
 
     project(HALF)
 
-    forward_loop(NB, 2 * NB, (0,))
+    forward_loop(8, 16, (0,))
+    forward_loop(8, 16, (1, 2))
 
     row = own_rows(cell_ref[...])
     block = steps_of(row, 256, 9)
@@ -486,26 +487,22 @@
             part = dg(nw[...], qkv[:, col(n, g)], TN)
             src[:, n * width : (n + 1) * width] = part.astype(BF16)
 
-    back_loop(0, 16, 0)
+    hidden_grads()
+    sum_e.step()
+    back_loop(0, 8, 0)
+    sum_e.step()
+    back_loop(8, 16, 0)
+    sum_e.step()
     weight_grad(src_a, 0)
     sum_a.step()
-    forward_loop(8, 16, (1, 2))
-    sum_a.step()
-    hidden_grads()
-    sum_e.step()
     back_loop(0, 8, 1)
-    sum_a.step()
     sum_e.step()
     back_loop(8, 16, 1)
     sum_a.step()
+    sum_e.step()
     weight_grad(src_b, 1)
     sum_b.step()
-    sum_e.step()
-    back_loop(0, 8, 2)
-    sum_a.step()
-    sum_b.step()
-    sum_e.step()
-    back_loop(8, 16, 2)
+    back_loop(0, 16, 2)
     sum_a.step()
     sum_e.step()
     weight_grad(src_c, 2)
@@ -568,26 +565,29 @@
 
     project_back(HALF)
     sum_a.step()
-    sum_b.step()
     sum_e.step()
     second_windows(0, 4, 0)
     sum_c.step()
+    second_windows(4, 8, 1)
     sum_b.step()
-    second_windows(4, 8, 1)
+    sum_a.step()
+    project_back(0)
+    sum_e.step()
+    first_windows(0, 4, 0)
     sum_c.step()
     sum_b.step()
-    sum_e.step()
-    project_back(0)
+    first_windows(4, 8, 1)
+    sum_a.step()
+    sum_c.step()
+    sum_b.step()
     sum_c.step()
     sum_b.step()
     sum_a.step()
-    first_windows(0, 4, 0)
-    sum_c.step()
-    sum_e.step()
-    first_windows(4, 8, 1)
     sum_c.step()
     sum_b.step()
     sum_c.step()
+    sum_a.step()
+    sum_b.step()
     sum_c.step()
     finish(outs)
 

time: 110 us -> 107 us (0.973)
  Pallas kernels: 109 us -> 106 us
    pallas_call x1, Pallas kernels: 102 us -> 99.9 us  [fused_call(): pl.pallas_call(fused_kernel, out_shape=(SDS(x.shape, BF16), SDS((768, D),...]
where the time goes in v5:
time: 107 us
  Pallas kernels  106 us (99%)
    pallas_call x1, Pallas kernels, fused_call(): pl.pallas_call(fused_kernel, out_shape=(SDS(x.shape, BF16), SDS((768, D),...  99.9 us
    pallas_call x1, Pallas kernels, place_call(): pl.pallas_call(place_kernel, grid=(4,), out_shape=(SDS(gx.shape, BF16), S...  6.39 us

profile of v5, /device:TPU:1, one launch (start us, length us, event | category | flops | bytes accessed | tf_op | source)
XLA Modules:
  0.0 107.1 jit_solution(16457514877617125695)
XLA Ops:
  0.6 99.9 %fused.1 = (bf16[2,48,24,512]{3,2,1,0:T(8,128)(2,1)}, bf16[768,512]{1,0:T(8,128)(2,1)}, bf16[512,768]{1,0:T(8,128)(2,1)}, bf16[512,384]{1,0:T(8,128)(2,1)}, bf16...) custom-call(bf16[2,48,24,512]{3,2,1,0:T(8,128)(2,1)} %x_hbm.1, bf16[80,1024]{1,0:T(8,128)(2,1)} %bitcast.5, ...), custom_call_target="tpu_custom_call" | custom-call | tf_op jit(solution)/shard_map/fused/pallas_call | solution.py:650
  100.6 6.4 %place.1 = (bf16[2,48,24,512]{3,2,1,0:T(8,128)(2,1)}, f32[512,1536]{1,0:T(8,128)}, f32[512,512]{1,0:T(8,128)}, f32[80,512]{1,0:T(8,128)}, f32[1,512]{1,0:T(1,128)}) custom-call(bf16[2,48,24,512]{3,2,1,0:T(8,128)(2,1)} %get-tuple-element.16.gx_ref, bf16[768,512]{1,0:T(8,128)(2,1)} %get-tuple-element.17.arrive_ref, bf16[512,768]{1,0:T(8,128)(2,1)} %get-tuple-element.18.qa_ref, ...), custom_call_target="tpu_custom_call" | custom-call | tf_op jit(solution)/shard_map/place/pallas_call | solution.py:683

commit v6 on v5

--- a/solution.py
+++ b/solution.py
@@ -102,7 +102,7 @@
 
 NB = 8
 HALF = NB * WT
-GROUPS = ((0, 4), (4, 2), (6, 2))
+GROUPS = ((0, 4), (4, 4))
 ER = 640
 
 
@@ -257,20 +257,19 @@
 
 PLAN_E = (ER, D, True, 2, 2, True)
 PLAN_4 = (D, 768, True, 4, 1, False)
-PLAN_2 = (D, 384, False, 4, 1, False)
-PLAN_2Y = (D, 384, False, 4, 1, True)
+PLAN_4Y = (D, 768, True, 4, 1, True)
 
 
 def fused_kernel(
     x_hbm, pts_ref, slot_ref, weight_ref, count_ref, cell_ref, gain_ref, wqkv_hbm, wout_hbm,
     wdec_ref,
-    gx_hbm, arrive_ref, qa_ref, qb_ref, qc_ref, e_ref,
+    gx_hbm, arrive_ref, qa_ref, qb_ref, e_ref,
     xv, wqkv, wout, load_sem, store_sem,
     sent, arr, asend, arecv, first, halo, edge, hsems,
-    xw, nw, qkv, probs_a, probs_b, probs_c, att, oh, marr, gtt, dhf, dhb, datt, hid, dnf,
-    src_a, src_b, src_c, src_e,
-    a0, a1, a2, a3, a4, a5, b0, b1, b2, b3, b4, b5, c0, c1, c2, c3, c4, c5, e0, e1, e2, e3, e4, e5,
-    sems_a, sems_b, sems_c, sems_e,
+    xw, nw, qkv, probs_a, probs_b, att, oh, marr, gtt, dhf, dhb, datt, hid, dnf,
+    src_a, src_b, src_e,
+    a0, a1, a2, a3, a4, a5, b0, b1, b2, b3, b4, b5, e0, e1, e2, e3, e4, e5,
+    sems_a, sems_b, sems_e,
 ):
     lat, lon = spot()
     core = lax.rem(lon, 2)
@@ -294,10 +293,9 @@
         pl.semaphore_signal(barrier, inc=1, device_id=dev, device_id_type=MESH)
 
     sum_a = Sum(src_a, qa_ref, PLAN_4, (a0, a1, a2, a3, a4, a5), sems_a)
-    sum_b = Sum(src_b, qb_ref, PLAN_2, (b0, b1, b2, b3, b4, b5), sems_b)
-    sum_c = Sum(src_c, qc_ref, PLAN_2Y, (c0, c1, c2, c3, c4, c5), sems_c)
+    sum_b = Sum(src_b, qb_ref, PLAN_4Y, (b0, b1, b2, b3, b4, b5), sems_b)
     sum_e = Sum(src_e, e_ref, PLAN_E, (e0, e1, e2, e3, e4, e5), sems_e)
-    probs = (probs_a, probs_b, probs_c)
+    probs = (probs_a, probs_b)
 
     pts = jnp.concatenate([pts_ref[:, n * 256 : (n + 1) * 256] for n in range(4)], axis=0)
     lane = lax.broadcasted_iota(jnp.int32, (1, CAP), 1)
@@ -357,7 +355,7 @@
     project(0)
 
     masks, picks = {}, {}
-    for n in (4, 2):
+    for n in (4,):
         head = lax.broadcasted_iota(jnp.int32, (1, n * HD), 1) // HD
         masks[n] = [jnp.where(head == a, 1.0, 0.0).astype(BF16) for a in range(n)]
         picks[n] = [head == a for a in range(n)]
@@ -399,7 +397,7 @@
             forward(w, some)
 
     forward_loop(0, 8, (0,))
-    forward_loop(0, 8, (1, 2))
+    forward_loop(0, 8, (1,))
     in_copy.wait()
 
     @pl.loop(0, NB)
@@ -419,7 +417,7 @@
     project(HALF)
 
     forward_loop(8, 16, (0,))
-    forward_loop(8, 16, (1, 2))
+    forward_loop(8, 16, (1,))
 
     row = own_rows(cell_ref[...])
     block = steps_of(row, 256, 9)
@@ -497,16 +495,11 @@
     sum_a.step()
     back_loop(0, 8, 1)
     sum_e.step()
+    sum_a.step()
     back_loop(8, 16, 1)
+    sum_e.step()
     sum_a.step()
-    sum_e.step()
     weight_grad(src_b, 1)
-    sum_b.step()
-    back_loop(0, 16, 2)
-    sum_a.step()
-    sum_e.step()
-    weight_grad(src_c, 2)
-    sum_c.step()
     sum_b.step()
 
     sub = sub_iota((WA, 8, D))
@@ -564,36 +557,31 @@
         outs[-1].start()
 
     project_back(HALF)
+    sum_b.step()
+    sum_e.step()
+    sum_a.step()
+    second_windows(0, 4, 0)
+    second_windows(4, 8, 1)
     sum_a.step()
     sum_e.step()
-    second_windows(0, 4, 0)
-    sum_c.step()
-    second_windows(4, 8, 1)
+    project_back(0)
     sum_b.step()
     sum_a.step()
-    project_back(0)
+    first_windows(0, 4, 0)
+    first_windows(4, 8, 1)
+    sum_b.step()
     sum_e.step()
-    first_windows(0, 4, 0)
-    sum_c.step()
-    sum_b.step()
-    first_windows(4, 8, 1)
-    sum_a.step()
-    sum_c.step()
-    sum_b.step()
-    sum_c.step()
     sum_b.step()
     sum_a.step()
-    sum_c.step()
     sum_b.step()
-    sum_c.step()
+    sum_b.step()
     sum_a.step()
     sum_b.step()
-    sum_c.step()
     finish(outs)
 
 
 def place_kernel(
-    gx_ref, arrive_ref, qa_ref, qb_ref, qc_ref, e_ref, edec_ref, wqkv_ref, gain_ref,
+    gx_ref, arrive_ref, qa_ref, qb_ref, e_ref, edec_ref, wqkv_ref, gain_ref,
     out_ref, gqkv_ref, gout_ref, gdec_ref, ggain_ref, gains,
 ):
     sub = sub_iota((WA, 8, D))
@@ -605,7 +593,7 @@
             edge = jnp.where(sub < 6, new.reshape(WA, 8, D), x[:, 0:8])
             out_ref[lev, at] = jnp.concatenate([edge, x[:, 8:24]], 1).astype(BF16)
     acc = jnp.zeros((128, 128), F32)
-    for (first, count), q_ref in zip(GROUPS, (qa_ref, qb_ref, qc_ref)):
+    for (first, count), q_ref in zip(GROUPS, (qa_ref, qb_ref)):
         width = count * HD
         for n in range(3):
             cols = slice(n * D + first * HD, n * D + first * HD + width)
@@ -650,22 +638,22 @@
     return pl.pallas_call(
         fused_kernel,
         out_shape=(
-            SDS(x.shape, BF16), SDS((768, D), BF16), SDS((D, 768), BF16), SDS((D, 384), BF16),
-            SDS((D, 384), BF16), SDS((ER, D), BF16),
+            SDS(x.shape, BF16), SDS((768, D), BF16), SDS((D, 768), BF16), SDS((D, 768), BF16),
+            SDS((ER, D), BF16),
         ),
         in_specs=[ANY, VM, VM, VM, SM, VM, VM, ANY, ANY, VM],
-        out_specs=(ANY, VM, VM, VM, VM, VM),
+        out_specs=(ANY, VM, VM, VM, VM),
         scratch_shapes=[
             vm(2, 48, 24, D), vm(D, 3 * D), vm(D, D), DMA((3,)), DMA((3,)),
             vm(7, C, CAP), vm(BANDS, C, CAP), DMA((7,)), DMA((7,)),
             vm(768, D), vm(768, D), vm(768, D), DMA((8,)),
             vm(TOK, D), vm(TOK, D), vm(TOK, 3 * D),
-            vm(TOK, 4 * WT), vm(TOK, 2 * WT), vm(TOK, 2 * WT), vm(TOK, D),
+            vm(TOK, 4 * WT), vm(TOK, 4 * WT), vm(TOK, D),
             vm(256, BANDS * CAP), vm(9 * C, BANDS * CAP), vm(C, TOK), vm(TOK, D, dtype=F32),
             vm(TOK, D), vm(TOK, D), vm(TOK, D), vm(HALF, D, dtype=F32),
-            vm(D, 768), vm(D, 384), vm(D, 384), vm(ER, D),
-            *sum_bufs(PLAN_4), *sum_bufs(PLAN_2), *sum_bufs(PLAN_2), *sum_bufs(PLAN_E),
-            DMA((2, 17)), DMA((2, 17)), DMA((2, 17)), DMA((2, 17)),
+            vm(D, 768), vm(D, 768), vm(ER, D),
+            *sum_bufs(PLAN_4), *sum_bufs(PLAN_4Y), *sum_bufs(PLAN_E),
+            DMA((2, 17)), DMA((2, 17)), DMA((2, 17)),
         ],
         compiler_params=pltpu.CompilerParams(
             vmem_limit_bytes=62 << 20, collective_id=0, has_side_effects=True
@@ -674,7 +662,7 @@
     )(x, pts_t, slots, weights, counts, cells, gain, w_qkv, w_out, w_dec_t)
 
 
-def place_call(gx, arriving, qa, qb, qc, e, w_qkv, gain):
+def place_call(gx, arriving, qa, qb, e, w_qkv, gain):
     def rows(lanes):
         return pl.BlockSpec((128, lanes), lambda i: (i, 0))
 
@@ -688,14 +676,14 @@
             SDS((1, D), F32),
         ),
         in_specs=[
-            grid_rows, pl.BlockSpec((192, D), lambda i: (i, 0)), rows(768), rows(384), rows(384),
+            grid_rows, pl.BlockSpec((192, D), lambda i: (i, 0)), rows(768), rows(768),
             rows(D), pl.BlockSpec((128, D), lambda i: (4, 0)), rows(3 * D), across,
         ],
         out_specs=(grid_rows, rows(3 * D), rows(D), pl.BlockSpec((C, D), lambda i: (0, 0)), across),
         scratch_shapes=[pltpu.VMEM((D, 128), F32)],
         compiler_params=pltpu.CompilerParams(vmem_limit_bytes=60 << 20),
         name="place",
-    )(gx, arriving, qa, qb, qc, e, e, w_qkv, gain)
+    )(gx, arriving, qa, qb, e, e, w_qkv, gain)
 
 
 def body(

time: 107 us -> 110 us (1.028)
  Pallas kernels: 106 us -> 109 us
    pallas_call x1, Pallas kernels: 99.9 us -> 103 us  [fused_call(): pl.pallas_call(fused_kernel, out_shape=(SDS(x.shape, BF16), SDS((768, D),...]
where the time goes in v6:
time: 110 us
  Pallas kernels  109 us (99%)
    pallas_call x1, Pallas kernels, fused_call(): pl.pallas_call(fused_kernel, out_shape=(SDS(x.shape, BF16), SDS((768, D),...  103 us
    pallas_call x1, Pallas kernels, place_call(): pl.pallas_call(place_kernel, grid=(4,), out_shape=(SDS(gx.shape, BF16), S...  6.37 us

profile of v6, /device:TPU:1, one launch (start us, length us, event | category | flops | bytes accessed | tf_op | source)
XLA Modules:
  0.0 110.2 jit_solution(8360690208043882465)
XLA Ops:
  0.6 103.0 %fused.1 = (bf16[2,48,24,512]{3,2,1,0:T(8,128)(2,1)}, bf16[768,512]{1,0:T(8,128)(2,1)}, bf16[512,768]{1,0:T(8,128)(2,1)}, bf16[512,768]{1,0:T(8,128)(2,1)}, bf16[640,512]{1,0:T(8,128)(2,1)}) custom-call(bf16[2,48,24,512]{3,2,1,0:T(8,128)(2,1)} %x_hbm.1, bf16[80,1024]{1,0:T(8,128)(2,1)} %bitcast.5, s32[8,512]{1,0:T(8,128)} %slot_ref.1, f32[8,512]{1,0:T(8,128)} %weight_ref.1, ...), custom_call_target="tpu_custom_call" | custom-call | tf_op jit(solution)/shard_map/fused/pallas_call | solution.py:638
  103.7 6.4 %place.1 = (bf16[2,48,24,512]{3,2,1,0:T(8,128)(2,1)}, f32[512,1536]{1,0:T(8,128)}, f32[512,512]{1,0:T(8,128)}, f32[80,512]{1,0:T(8,128)}, f32[1,512]{1,0:T(1,128)}) custom-call(bf16[2,48,24,512]{3,2,1,0:T(8,128)(2,1)} %get-tuple-element.15.gx_ref, bf16[768,512]{1,0:T(8,128)(2,1)} %get-tuple-element.16.arrive_ref, bf16[512,768]{1,0:T(8,128)(2,1)} %get-tuple-element.17.qa_ref, ...), custom_call_target="tpu_custom_call" | custom-call | tf_op jit(solution)/shard_map/place/pallas_call | solution.py:671

commit v7 on v2

--- a/solution.py
+++ b/solution.py
@@ -298,9 +298,6 @@
         live = lane < count_ref[d]
         return jnp.where(live, weight_ref[pl.ds(d, 1), :] * rows, 0.0).astype(BF16)
 
-    for s, o in enumerate(others):
-        sent[s] = rows_for(o)
-    arr[lat] = rows_for(lat)
     loads[0].wait()
 
     @pl.loop(0, NB)
@@ -313,10 +310,11 @@
     pl.semaphore_wait(barrier, len(peers))
     in_copy = remote(first, halo, hsems.at[0], hsems.at[1], device(lat, west))
     in_copy.start()
-    copies = start([
-        remote(sent.at[s], arr.at[lat], asend.at[s], arecv.at[s], device(o, lon))
-        for s, o in enumerate(others)
-    ])
+    copies = []
+    for s, o in enumerate(others):
+        sent[s] = rows_for(o)
+        copies += start([remote(sent.at[s], arr.at[lat], asend.at[s], arecv.at[s], device(o, lon))])
+    arr[lat] = rows_for(lat)
 
     gain = gain_ref[...]
 
@@ -386,6 +384,11 @@
     def _(w):
         forward(w)
 
+    row = own_rows(cell_ref[...])
+    block = steps_of(row, 256, 9)
+    place = row - block * 256
+    for i in range(BANDS):
+        oh[:, i * CAP : (i + 1) * CAP] = onehot(place[i : i + 1, :], 256)
     in_copy.wait()
 
     @pl.loop(0, NB)
@@ -408,11 +411,6 @@
     def _(w):
         forward(w)
 
-    row = own_rows(cell_ref[...])
-    block = steps_of(row, 256, 9)
-    place = row - block * 256
-    for i in range(BANDS):
-        oh[:, i * CAP : (i + 1) * CAP] = onehot(place[i : i + 1, :], 256)
     finish(copies)
     for i in range(BANDS):
         part = arr[i]

time: 107 us -> 107 us (level)
  no operation moved by 1% of the time
where the time goes in v7:
time: 107 us
  Pallas kernels  106 us (99%)
    pallas_call x1, Pallas kernels, fused_call(): pl.pallas_call(fused_kernel, out_shape=(SDS(x.shape, BF16), SDS((768, D),...  99.9 us
    pallas_call x1, Pallas kernels, place_call(): pl.pallas_call(place_kernel, grid=(4,), out_shape=(SDS(gx.shape, BF16), S...  6.48 us

profile of v7, /device:TPU:1, one launch (start us, length us, event | category | flops | bytes accessed | tf_op | source)
XLA Modules:
  0.0 107.2 jit_solution(14403697229089729200)
XLA Ops:
  0.6 99.9 %fused.1 = (bf16[2,48,24,512]{3,2,1,0:T(8,128)(2,1)}, bf16[768,512]{1,0:T(8,128)(2,1)}, bf16[512,768]{1,0:T(8,128)(2,1)}, bf16[512,384]{1,0:T(8,128)(2,1)}, bf16...) custom-call(bf16[2,48,24,512]{3,2,1,0:T(8,128)(2,1)} %x_hbm.1, bf16[80,1024]{1,0:T(8,128)(2,1)} %bitcast.5, ...), custom_call_target="tpu_custom_call" | custom-call | tf_op jit(solution)/shard_map/fused/pallas_call | solution.py:620
  100.6 6.5 %place.1 = (bf16[2,48,24,512]{3,2,1,0:T(8,128)(2,1)}, f32[512,1536]{1,0:T(8,128)}, f32[512,512]{1,0:T(8,128)}, f32[80,512]{1,0:T(8,128)}, f32[1,512]{1,0:T(1,128)}) custom-call(bf16[2,48,24,512]{3,2,1,0:T(8,128)(2,1)} %get-tuple-element.16.gx_ref, bf16[768,512]{1,0:T(8,128)(2,1)} %get-tuple-element.17.arrive_ref, bf16[512,768]{1,0:T(8,128)(2,1)} %get-tuple-element.18.qa_ref, ...), custom_call_target="tpu_custom_call" | custom-call | tf_op jit(solution)/shard_map/place/pallas_call | solution.py:653
